TPU v7x, 32 devices: a whole 2x2x4 slice. The times are simulated.
32 devices in a mesh: wa: 2 (over x), uv: 16 (over z, y, core).
Axes of the slice: x: 2, y: 2, z: 4, core: 2. Of those that a mesh axis runs over, the one named last changes fastest.
Arguments:
- visibility: bfloat16 [1536, 2, 256], P(('wa', 'uv')), may hold values from -6 to 6
- coords: bfloat16 [1536, 2, 256], P(('wa', 'uv')), may hold values from -24 to 24
- tile_row: int32 [1536, 1], P(('wa', 'uv')), may hold values from 0 to 63; in each aligned block of 48 rows (0 to 47, 48 to 95, ...) at most 2 rows name the same one
- col_offset: int32 [1536], P(('wa', 'uv')), may hold values from 0 to 4032
- live_count: int32 [2, 16], P('wa', 'uv'), may hold values from 1 to 48, 480 in all within a row
Outputs:
- sky_image: float32 [4096, 4096], P('uv', 'wa')
Inputs may be any that keep to these rules, and one draw needn't show every extreme that they name: `tile_row`: within the blocks of one device, at most 2 name the same tile row, and some device reaches 2. A device's live blocks are its first live_count ones; in each w group the 16 counts sum to 480, and the largest count is 48.
All inputs are finite; a program needn't handle non-finite values.
Results may differ from a plain program's by a relative error of at most 0.0069.
Values may be sent and summed in bfloat16 or wider, within the bound.
A program may use at most 128 MiB of HBM per device.

v0:
```python
import functools
import math

import jax
import jax.numpy as jnp
import ml_dtypes
import numpy as np
from jax import lax
from jax.experimental import pallas as pl
from jax.experimental.pallas import tpu as pltpu
from jax.sharding import PartitionSpec as P

G = 4096
SUB = 64
UNROLL = 8
plane_step = 6.0
full_turn = 2.0 * math.pi
BF = ml_dtypes.bfloat16


def turn_poly():
    nodes = np.cos(np.pi * (np.arange(256) + 0.5) / 256)
    z = (nodes + 1.0) / 8.0
    f = np.sqrt(z)
    cos_c = np.polynomial.chebyshev.cheb2poly(
        np.polynomial.chebyshev.chebfit(nodes, np.cos(2 * np.pi * f), 7)
    )
    sin_c = np.polynomial.chebyshev.cheb2poly(
        np.polynomial.chebyshev.chebfit(nodes, np.sin(2 * np.pi * f) / f, 7)
    )
    base = np.polynomial.Polynomial([-1.0, 8.0])
    out = []
    for coefs in (cos_c, sin_c):
        total = np.polynomial.Polynomial([0.0])
        for c in coefs[::-1]:
            total = total * base + c
        out.append([float(c) for c in total.coef])
    return out


COS_C, SIN_C = turn_poly()


def cos_sin_turns(turns):
    f = turns - jnp.round(turns)
    z = f * f
    c = jnp.full_like(z, COS_C[-1])
    for k in COS_C[-2::-1]:
        c = c * z + k
    s = jnp.full_like(z, SIN_C[-1])
    for k in SIN_C[-2::-1]:
        s = s * z + k
    return c, s * f


def factor_table():
    o = np.arange(SUB) - SUB // 2
    ang = full_turn / SUB * np.mod(o[:, None] * o[None, :], SUB)
    return np.cos(ang).astype(BF), (-np.sin(ang)).astype(BF)


def factor_matrix():
    fr, fi = factor_table()
    return np.block([[fr, -fi], [fi, fr]]).astype(BF)


def head_matrices():
    l0 = np.arange(64)[:, None]
    out = []
    for core in range(2):
        columns = []
        for source in range(2):
            t = (2 * np.arange(32) + (core ^ source))[None, :]
            ang = full_turn / 64 * np.mod(l0 * t, 64)
            c, s = np.cos(ang), np.sin(ang)
            columns.append(np.block([[c, -s], [s, c]]))
        out.append(np.concatenate(columns, axis=1))
    return np.stack(out).astype(BF)


def tail_matrices():
    l0 = np.arange(64)[:, None, None]
    p = np.arange(64)[None, :, None]
    l1 = np.arange(64)[None, None, :]
    ang = full_turn / G * np.mod(p * (l0 + 64 * l1), G)
    sign = 1.0 - 2.0 * ((p + l0) % 2)
    c, s = np.cos(ang) * sign, np.sin(ang) * sign
    top = np.concatenate([c, s], axis=2)
    bottom = np.concatenate([-s, c], axis=2)
    return np.concatenate([top, bottom], axis=1).astype(BF)


def split_tail(parts):
    whole = tail_matrices().reshape(64, 128, 2, parts, 64 // parts)
    return np.ascontiguousarray(whole.transpose(3, 0, 1, 2, 4)).reshape(parts, 64, 128, -1)


def gather_kernel(far, near, x_ref, out_ref, z_send, z_recv, y_send, y_recv, c_send, c_recv):
    me = lax.axis_index("uv")
    c = lax.rem(me, 2)
    b = lax.rem(me // 2, near)
    a = me // (2 * near)

    def at(da, db, dc):
        return (
            lax.rem(a + da + far, far) * near + lax.rem(b + db + near, near)
        ) * 2 + lax.rem(c + dc, 2)

    peers = [at(d, 0, 0) for d in range(1, far)]
    peers += [at(0, e, 0) for e in range(1, near)] + [at(0, 0, 1)]
    barrier = pltpu.get_barrier_semaphore()
    for peer in peers:
        pl.semaphore_signal(
            barrier, inc=1, device_id={"uv": peer}, device_id_type=pl.DeviceIdType.MESH
        )
    pl.semaphore_wait(barrier, len(peers))

    def copy(source, slot, target, send, recv):
        return pltpu.make_async_remote_copy(
            src_ref=source,
            dst_ref=out_ref.at[slot],
            send_sem=send,
            recv_sem=recv,
            device_id={"uv": target},
            device_id_type=pl.DeviceIdType.MESH,
        )

    sent = []

    def send(source, slot, target, send_sem, recv_sem):
        one = copy(source, slot, target, send_sem, recv_sem)
        one.start()
        sent.append(one)

    for d in range(1, far):
        send(x_ref, me, at(d, 0, 0), z_send.at[d], z_recv.at[d])
    for d in range(far):
        slot = at(-d, 0, 0)
        source = x_ref if d == 0 else out_ref.at[slot]
        if d > 0:
            copy(x_ref, slot, me, z_send.at[d], z_recv.at[d]).wait_recv()
        for e in range(1, near):
            k = d * near + e
            send(source, slot, at(0, e, 0), y_send.at[k], y_recv.at[k])
        k = d * near
        send(source, slot, at(0, 0, 1), c_send.at[k], c_recv.at[k])
        if d == 0:
            out_ref[me] = x_ref[...]
    for d in range(far):
        for e in range(1, near):
            k = d * near + e
            slot = at(-d, -e, 0)
            copy(x_ref, slot, me, y_send.at[k], y_recv.at[k]).wait_recv()
            send(out_ref.at[slot], slot, at(0, 0, 1), c_send.at[k], c_recv.at[k])
    for d in range(far):
        for e in range(near):
            k = d * near + e
            copy(x_ref, at(-d, -e, 1), me, c_send.at[k], c_recv.at[k]).wait_recv()
    for one in sent:
        one.wait_send()


def gather_all(packed, uv_count):
    chips = uv_count // 2
    near = 1 << ((chips.bit_length() - 1) // 2)
    far = chips // near
    sems = [far] * 2 + [far * near] * 4
    return pl.pallas_call(
        functools.partial(gather_kernel, far, near),
        out_shape=jax.ShapeDtypeStruct((uv_count,) + packed.shape, packed.dtype),
        in_specs=[pl.BlockSpec(memory_space=pltpu.VMEM)],
        out_specs=pl.BlockSpec(memory_space=pltpu.VMEM),
        scratch_shapes=[pltpu.SemaphoreType.DMA((n,)) for n in sems],
        compiler_params=pltpu.CompilerParams(
            collective_id=0, has_side_effects=True, vmem_limit_bytes=24 * 1024 * 1024
        ),
    )(packed)


def grid_kernel(
    width, blocks, tiles, counts, data_ref, cols_ref, moff_ref, mf_ref, d_ref,
    keep_ref, give_ref, acc, rows_f, phase, mine,
):
    devices = data_ref.shape[0]
    acc[...] = jnp.zeros_like(acc)
    core = counts[devices]

    def spread(j, found):
        rows_f[j] = data_ref[j].astype(jnp.float32)
        for h in range(2):
            turn = jnp.bitwise_and((cols_ref[j] - G // 2) * moff_ref[h : h + 1, :], G - 1)
            pc, ps = cos_sin_turns(turn.astype(jnp.float32) * (1.0 / G))
            phase[j, 2 * h] = pc
            phase[j, 2 * h + 1] = ps

        def pick(i, n):
            mine[n] = j * blocks + i
            return n + jnp.where(lax.rem(tiles[j * blocks + i], 2) == core, 1, 0)

        return lax.fori_loop(0, counts[j], pick, found)

    total = lax.fori_loop(0, devices, spread, 0)
    k_len = data_ref.shape[2]
    offs = lax.broadcasted_iota(jnp.int32, (8, k_len), 0).astype(jnp.float32)
    fine = offs * (1.0 / SUB)
    coarse = (offs - 4.0) * (8.0 / SUB)
    scale = 1.0 / math.sqrt(k_len)

    def expand(pr, pi, c1, s1):
        res, ims = [], []
        for a in range(8):
            ar, ai = pr[a : a + 1, :], pi[a : a + 1, :]
            res.append(ar * c1 - ai * s1)
            ims.append(ar * s1 + ai * c1)
        return jnp.concatenate(res + ims, axis=0).astype(jnp.bfloat16)

    def step(it, carry):
        lefts, rights, index = [], [], []
        for k in range(UNROLL):
            n = it * UNROLL + k
            g = jnp.where(n < total, mine[n], 0)
            j = g // blocks
            i = g - j * blocks
            index.append((g, j, i))
            keep = jnp.where(n < total, scale, 0.0)
            vr, vi, u, v = (rows_f[j, pl.ds(q * blocks + i, 1), :] for q in range(4))
            c1, s1 = cos_sin_turns(fine * u)
            c8, s8 = cos_sin_turns(coarse * u)
            lefts.append(
                expand((vr * c8 - vi * s8) * keep, (vr * s8 + vi * c8) * keep, c1, s1)
            )
            d1, t1 = cos_sin_turns(fine * v)
            d8, t8 = cos_sin_turns(coarse * v)
            rights.append(expand(d8, t8, d1, t1))
        parts = []
        for k in range(UNROLL):
            s = lax.dot_general(
                lefts[k], rights[k], (((1,), (1,)), ((), ())), preferred_element_type=jnp.float32
            ).astype(jnp.bfloat16)
            c = jnp.dot(mf_ref[...], s, preferred_element_type=jnp.float32).astype(jnp.bfloat16)
            parts.append(jnp.concatenate([c[:SUB], c[SUB:]], axis=1))
        joined = jnp.concatenate(parts, axis=0)
        for h in range(2):
            out = jnp.dot(
                joined,
                d_ref[:, 2 * h * width : 2 * (h + 1) * width],
                preferred_element_type=jnp.float32,
            )
            for k in range(UNROLL):
                g, j, i = index[k]
                pr = phase[j, 2 * h, pl.ds(i, 1), :]
                pi = phase[j, 2 * h + 1, pl.ds(i, 1), :]
                hr = out[k * SUB : (k + 1) * SUB, :width]
                hi = out[k * SUB : (k + 1) * SUB, width:]
                rows = pl.ds(pl.multiple_of(tiles[g] // 2 * SUB, SUB), SUB)
                acc[2 * h, rows, :] += hr * pr - hi * pi
                acc[2 * h + 1, rows, :] += hr * pi + hi * pr
        return carry

    lax.fori_loop(0, (total + UNROLL - 1) // UNROLL, step, 0)

    half_rows = acc.shape[1] // SUB
    for h, ref in enumerate((keep_ref, give_ref)):
        for c in range(2):
            ref[c] = acc[2 * h + c].astype(jnp.bfloat16).reshape(half_rows, SUB, width)


def on_device(visibility, coords, tile_row, col_offset, live_count):
    uv_count = lax.axis_size("uv")
    wa_count = lax.axis_size("wa")
    uv_index = lax.axis_index("uv")
    wa_index = lax.axis_index("wa")
    blocks = visibility.shape[0]
    k_len = visibility.shape[2]
    width = G // uv_count
    core = jnp.mod(uv_index, 2)
    numbers = jnp.stack(
        [
            tile_row[:, 0],
            col_offset // SUB,
            jnp.mod(col_offset, SUB),
            jnp.broadcast_to(live_count[0], (blocks,)),
        ]
    )
    numbers = jnp.pad(numbers, ((0, 12), (0, k_len - blocks))).astype(jnp.bfloat16)
    packed = jnp.concatenate(
        [visibility[:, 0], visibility[:, 1], coords[:, 0], coords[:, 1], numbers], axis=0
    )
    all_data = gather_all(packed, uv_count)
    came_numbers = all_data[:, 4 * blocks : 4 * blocks + 4, :blocks].astype(jnp.int32)
    tiles = came_numbers[:, 0].reshape(-1)
    cols = (came_numbers[:, 1] * SUB + came_numbers[:, 2])[:, :, None]
    counts = jnp.concatenate([came_numbers[:, 3, 0], core[None]])

    m_off = uv_index * width + jnp.arange(width) - G // 2
    partner = uv_index + 1 - 2 * core
    m_both = jnp.stack([m_off, partner * width + jnp.arange(width) - G // 2])

    fr, fi = factor_table()
    fr, fi = fr.astype(np.float32), fi.astype(np.float32)
    qt = jnp.mod(jnp.arange(SUB)[:, None] * m_both.reshape(-1)[None, :], G).astype(jnp.float32)
    qc, qs = cos_sin_turns(qt * (1.0 / G))
    both = jnp.dot(
        jnp.asarray(np.block([[fr.T, -fi.T], [fi.T, fr.T]]) / SUB),
        jnp.concatenate([qc, qs], axis=0),
        precision=lax.Precision.HIGHEST,
    )
    dr, di = both[:SUB].reshape(SUB, 2, width), both[SUB:].reshape(SUB, 2, width)
    ddr = jnp.concatenate([dr, -di], axis=0)
    ddi = jnp.concatenate([di, dr], axis=0)
    d_table = jnp.concatenate(
        [jnp.stack([ddr, ddi], axis=2), jnp.stack([-ddi, ddr], axis=2)], axis=0
    ).reshape(4 * SUB, 4 * width).astype(jnp.bfloat16)

    rows = packed.shape[0]
    half_tiles = G // SUB // 2
    shape = (2, half_tiles, SUB, width)
    vmem = pl.BlockSpec(memory_space=pltpu.VMEM)
    smem = pl.BlockSpec(memory_space=pltpu.SMEM)
    own, give = pl.pallas_call(
        functools.partial(grid_kernel, width, blocks),
        out_shape=[jax.ShapeDtypeStruct(shape, jnp.bfloat16)] * 2,
        in_specs=[smem, smem, vmem, vmem, vmem, vmem, vmem],
        out_specs=[vmem, vmem],
        scratch_shapes=[
            pltpu.VMEM((4, G // 2, width), jnp.float32),
            pltpu.VMEM((uv_count, rows, k_len), jnp.float32),
            pltpu.VMEM((uv_count, 4, blocks, width), jnp.float32),
            pltpu.SMEM((uv_count * blocks + UNROLL,), jnp.int32),
        ],
        compiler_params=pltpu.CompilerParams(vmem_limit_bytes=48 * 1024 * 1024),
    )(tiles, counts, all_data, cols, m_both, jnp.asarray(factor_matrix()), d_table)
    came_half = lax.ppermute(give, "uv", [(n, n ^ 1) for n in range(uv_count)])
    half = jnp.concatenate([own, came_half], axis=0)

    first = jnp.dot(
        jnp.asarray(head_matrices())[core],
        half.reshape(2 * 64, 64 * width),
        preferred_element_type=jnp.float32,
    ).astype(jnp.bfloat16)
    first = first.reshape(2, 64, 64, width).transpose(1, 0, 2, 3).reshape(64, 128, width)
    share = 64 // wa_count
    depth = (wa_index.astype(jnp.float32) - (wa_count - 1) / 2.0) * plane_step
    y = m_off[None, :, None].astype(jnp.float32) / G
    tail = jnp.asarray(split_tail(wa_count))

    def shares_of(part, first):
        image = jnp.einsum("lxm,lxy->lmy", first, tail[part], preferred_element_type=jnp.float32)
        l1 = part * share + jnp.arange(share)[None, None, :]
        x = (jnp.arange(64)[:, None, None] + 64 * l1 - G // 2).astype(jnp.float32) / G
        depth_term = jnp.sqrt(1.0 - y**2 - x**2)
        sc, ss = cos_sin_turns(depth * (depth_term - 1.0))
        screened = (image[:, :, :share] * sc - image[:, :, share:] * ss) * (1.0 / G)
        return screened

    def in_order(screened):
        return screened.transpose(1, 2, 0).reshape(width, G // wa_count)

    if wa_count == 2:
        away = in_order(shares_of(1 - wa_index, first).astype(jnp.bfloat16))
        came = lax.ppermute(away, "wa", [(0, 1), (1, 0)])
        first, _ = lax.optimization_barrier((first, away))
        return in_order(shares_of(wa_index, first)) + came.astype(jnp.float32)
    parts = jnp.stack(
        [in_order(shares_of(part, first).astype(jnp.bfloat16)) for part in range(wa_count)], axis=1
    )
    came = lax.all_to_all(parts, "wa", split_axis=1, concat_axis=1)
    return jnp.sum(came.astype(jnp.float32), axis=1)


def solution(mesh):
    in_specs = (
        P(("wa", "uv"), None, None),
        P(("wa", "uv"), None, None),
        P(("wa", "uv"), None),
        P(("wa", "uv")),
        P("wa", "uv"),
    )
    return jax.shard_map(
        on_device, mesh=mesh, in_specs=in_specs, out_specs=P("uv", "wa"), check_vma=False
    )
```

profile of v0, /device:TPU:0, one launch (start us, length us, event | category | flops | bytes accessed | tf_op | source)
XLA Modules:
  0.0 137.0 jit_solution(5936726263031556262)
XLA Ops:
  0.0 0.0 copy-start.3
  0.0 0.0 copy-start.4
  0.0 0.0 copy-start.6
  0.0 0.0 copy-start.7
  0.0 1.4 %fusion.56 = f32[512,128]{0,1:T(8,128)S(1)} fusion(f32[128,64]{1,0:T(8,128)} %constant.165, s32[512]{0:T(512)S(1)} %bitcast.97), kind=kOutput, calls=%fused_computation.101 | convolution fusion | flops 51347456 | bytes 296960 | tf_op jit(solution)/shard_map/dot_general | solution.py:303
  1.4 1.4 fusion.22
  2.8 0.0 copy-done.3
  2.9 0.1 fusion.119
  2.9 0.0 copy-done.4
  3.0 0.1 fusion.118
  3.0 0.0 copy-done.6
  3.7 0.0 copy-done.7
  3.8 0.1 pad.25.clone
  3.9 0.1 maximum_maximum_fusion.1
  3.9 20.8 %shard_map.91.data_ref = bf16[16,208,256]{2,1,0:T(8,128)(2,1)S(1)} custom-call(bf16[208,256]{1,0:T(8,128)(2,1)S(1)} %constant_dynamic-update-slice_fusion.x_ref), custom_call_target="tpu_custom_call" | custom-call | tf_op jit(solution)/shard_map/pallas_call | solution.py:168
  24.7 0.4 slice_reduce_fusion
  25.2 0.1 concatenate.41
  25.3 0.1 concatenate.42
  25.5 0.0 copy-start.1
  25.6 0.5 copy.28
  26.1 0.4 convert_element_type.48.d_ref
  26.5 0.2 copy.29.cols_ref
  26.7 0.1 reshape_squeeze.3.tiles
  26.8 0.1 pad_add_fusion.1.counts
  26.8 0.0 copy-done.1
  26.8 60.9 %shard_map.92 = (bf16[2,32,64,256]{3,2,1,0:T(8,128)(2,1)S(1)}, bf16[2,32,64,256]{3,2,1,0:T(8,128)(2,1)}) custom-call(s32[768]{0:T(1024)S(1)} %reshape_squeeze.3.tiles, s32[17]{0:T(128)S(1)} %pad_add_fusion.1.counts, bf16[16,208,256]{2,1,0:T(8,128)(2,1)S(1)} %shard_map.91.data_ref, s32[16,48,1]{2,1,0:T(8,128)S(1)} %copy.29.cols_ref, ...), custom_call_target="tpu_custom_call" | custom-call | tf_op jit(solution)/shard_map/pallas_call | solution.py:320
  87.7 0.0 copy-start
  87.7 1.3 copy-done
  89.0 2.0 %collective-permute-start = (bf16[2,32,64,256]{3,2,1,0:T(8,128)(2,1)}, bf16[2,32,64,256]{3,2,1,0:T(8,128)(2,1)S(1)}, u32[]{:S(2)}, u32[]{:S(2)}) collective-permute-start(bf16[2,32,64,256]{3,2,1,0:T(8,128)(2,1)} %get-tuple-element.9), channel_id=1, source_target_pairs={{0,1},{1,0},{2,3},{3,2},{4,5},{5,4},{6,7},{7,6},{8,9},{9,8},{10,11... | collective-permute-start | bytes 6291464 | tf_op jit(solution)/shard_map/ppermute | solution.py:333
  91.1 3.9 %collective-permute-done = bf16[2,32,64,256]{3,2,1,0:T(8,128)(2,1)S(1)} collective-permute-done((bf16[2,32,64,256]{3,2,1,0:T(8,128)(2,1)}, bf16[2,32,64,256]{3,2,1,0:T(8,128)(2,1)S(1)}, u32[]{:S(2)}, u32[]{:S(2)}) %collective-permute-start) | collective-permute-done | bytes 2097184 | tf_op jit(solution)/shard_map/ppermute | solution.py:333
  95.1 2.0 %pad_maximum_fusion = bf16[4,32,64,256]{3,2,1,0:T(8,128)(2,1)S(1)} fusion(bf16[2,32,64,256]{3,2,1,0:T(8,128)(2,1)S(1)} %collective-permute-done, bf16[2,32,64,256]{3,2,1,0:T(8,128)(2,1)} %copy-done), kind=kLoop, calls=%fused_computation.2 | loop fusion | flops 2097152 | bytes 8388608 | tf_op jit(solution)/shard_map/concatenate | solution.py:334
  97.0 0.0 copy-start.5
  97.0 2.9 %copy.42 = bf16[16,8,64,256]{3,1,2,0:T(8,128)(2,1)S(1)} copy(bf16[16,8,64,256]{3,2,1,0:T(8,128)(2,1)S(1)} %bitcast.86) | data formatting | bytes 8388608
  99.9 0.0 copy-done.5
  99.9 1.2 convolution_convert_fusion
  101.2 1.2 copy.43
  102.4 0.6 bitcast_bitcast_fusion
  103.0 0.0 copy-start.2
  103.0 0.6 copy.30
  103.6 1.0 copy-done.2
  104.6 0.7 fusion.25
  105.3 3.6 %fusion.29 = bf16[256,32,64]{0,1,2:T(8,128)(2,1)S(1)} fusion(f32[64,256,64]{1,2,0:T(8,128)S(1)} %fusion.25, f32[64,32]{1,0:T(8,128)S(1)} %multiply_multiply_fusion.25, f32[256]{0:T(256)S(1)} %multiply_subtract_fusion, f32[]{:T(128)S(6)} %mul.248), kind=kLoop, calls=%fused_computation.56 | loop fusion | flops 20971520 | bytes 5252100 | tf_op jit(solution)/shard_map/transpose | solution.py:357
  108.9 0.6 copy.31
  109.5 0.1 collective-permute-start.1
  109.5 0.7 fusion.23
  110.3 3.3 %fusion.2 = f32[256,32,64]{0,1,2:T(8,128)S(1)} fusion(f32[64,256,64]{1,2,0:T(8,128)S(1)} %fusion.23, f32[64,32]{1,0:T(8,128)S(1)} %multiply_multiply_fusion.24, f32[256]{0:T(256)S(1)} %multiply_subtract_fusion, f32[]{:T(128)S(6)} %mul.248), kind=kLoop, calls=%fused_computation.8 | loop fusion | flops 20447232 | bytes 6300676 | tf_op jit(solution)/shard_map/transpose | solution.py:357
  113.6 1.2 copy.32
  114.8 20.2 %collective-permute-done.1 = bf16[256,2048]{0,1:T(8,128)(2,1)S(1)} collective-permute-done((bf16[256,2048]{0,1:T(8,128)(2,1)S(1)}, bf16[256,2048]{0,1:T(8,128)(2,1)S(1)}, u32[]{:S(2)}, u32[]{:S(2)}) %collective-permute-start.1) | collective-permute-done | bytes 1048608 | tf_op jit(solution)/shard_map/ppermute | solution.py:361
  135.0 0.2 bitcast_add_fusion
  135.2 1.8 %copy.33 = f32[256,2048]{1,0:T(8,128)} copy(f32[256,2048]{0,1:T(8,128)S(1)} %bitcast_add_fusion) | data formatting | bytes 4194304 | tf_op jit(solution)/shard_map/add | solution.py:363
  (28 shorter events, 0.3 us)
Async XLA Ops:
  0.0 2.8 %copy-start.3 = (bf16[48,2,256]{2,1,0:T(2,128)(2,1)S(1)}, bf16[48,2,256]{2,1,0:T(2,128)(2,1)}, u32[]{:S(2)}) copy-start(bf16[48,2,256]{2,1,0:T(2,128)(2,1)} %param.9) | copy-start | bytes 147460
  0.0 2.9 %copy-start.4 = (bf16[48,2,256]{2,1,0:T(2,128)(2,1)S(1)}, bf16[48,2,256]{2,1,0:T(2,128)(2,1)}, u32[]{:S(2)}) copy-start(bf16[48,2,256]{2,1,0:T(2,128)(2,1)} %param.10) | copy-start | bytes 147460
  0.0 3.0 %copy-start.6 = (s32[48]{0:T(128)S(1)}, s32[48]{0:T(128)}, u32[]{:S(2)}) copy-start(s32[48]{0:T(128)} %param.12) | copy-start | bytes 580
  0.0 3.7 %copy-start.7 = (s32[48,1]{0,1:T(1,128)S(1)}, s32[48,1]{0,1:T(1,128)}, u32[]{:S(2)}) copy-start(s32[48,1]{0,1:T(1,128)} %param.11) | copy-start | bytes 580
  25.5 1.4 %copy-start.1 = (bf16[128,128]{1,0:T(8,128)(2,1)S(1)}, bf16[128,128]{1,0:T(8,128)(2,1)}, u32[]{:S(2)}) copy-start(bf16[128,128]{1,0:T(8,128)(2,1)} %constant.155.clone.mf_ref) | copy-start | bytes 98308
  87.7 1.3 copy-start
  89.0 6.0 %collective-permute-start = (bf16[2,32,64,256]{3,2,1,0:T(8,128)(2,1)}, bf16[2,32,64,256]{3,2,1,0:T(8,128)(2,1)S(1)}, u32[]{:S(2)}, u32[]{:S(2)}) collective-permute-start(bf16[2,32,64,256]{3,2,1,0:T(8,128)(2,1)} %get-tuple-element.9), channel_id=1, source_target_pairs={{0,1},{1,0},{2,3},{3,2},{4,5},{5,4},{6,7},{7,6},{8,9},{9,8},{10,11... | collective-permute-start | bytes 6291464 | tf_op jit(solution)/shard_map/ppermute | solution.py:333
  97.0 2.9 %copy-start.5 = (bf16[2,128,128]{2,1,0:T(8,128)(2,1)S(1)}, bf16[2,128,128]{2,1,0:T(8,128)(2,1)}, u32[]{:S(2)}) copy-start(bf16[2,128,128]{2,1,0:T(8,128)(2,1)} %constant.156.clone) | copy-start | bytes 196612
  103.0 1.6 %copy-start.2 = (bf16[2,64,128,64]{2,3,1,0:T(8,128)(2,1)S(1)}, bf16[2,64,128,64]{2,3,1,0:T(8,128)(2,1)}, u32[]{:S(2)}) copy-start(bf16[2,64,128,64]{2,3,1,0:T(8,128)(2,1)} %constant.157.clone) | copy-start | bytes 6291460
  109.5 25.5 %collective-permute-start.1 = (bf16[256,2048]{0,1:T(8,128)(2,1)S(1)}, bf16[256,2048]{0,1:T(8,128)(2,1)S(1)}, u32[]{:S(2)}, u32[]{:S(2)}) collective-permute-start(bf16[256,2048]{0,1:T(8,128)(2,1)S(1)} %bitcast.89), channel_id=1, source_target_pairs={{0,16},{16,0},{1,17},{17,1},{2,18},{18,2},{3,19},{19,3},{4,20},{20... | collective-permute-start | bytes 3145736 | tf_op jit(solution)/shard_map/ppermute | solution.py:361
where the time goes:
time: 137 us
  Pallas kernels  81.6 us (60%)
  waiting for transfers between devices  24.1 us (18%)
  local copies, waits for them, and re-layouts  13.3 us (10%)
  other arithmetic  9.37 us (7%)
  matrix products  5.42 us (4%)
  starting transfers between devices  2.09 us (2%)
    pallas_call x1, Pallas kernels, on_device(): pl.pallas_call(functools.partial(grid_kernel, width, blocks), out_shape=[...  60.9 us
    pallas_call x1, Pallas kernels, gather_all(): pl.pallas_call(functools.partial(gather_kernel, far, near), out_shape=jax...  20.8 us
    ppermute x1, waiting for transfers between devices, on_device(): came = lax.ppermute(away, 'wa', [(0, 1), (1, 0)])  20.2 us
    transpose x2, other arithmetic, in_order(): return screened.transpose(1, 2, 0).reshape(width, G // wa_count)  6.85 us
    unnamed x23, local copies, waits for them, and re-layouts  6.49 us
    ppermute x1, waiting for transfers between devices, on_device(): came_half = lax.ppermute(give, 'uv', [(n, n ^ 1) for n in range(uv_count)])  3.94 us
  transfers between devices with their start and end apart: 2, of which 2 were waited for; matrix products, arithmetic and copies ran while one was open for 4% of the time, Pallas kernels for 0%

commit v1 on v0

v1 whole, which is shorter than its diff:
```python
import functools
import math

import jax
import jax.numpy as jnp
import ml_dtypes
import numpy as np
from jax import lax
from jax.experimental import pallas as pl
from jax.experimental.pallas import tpu as pltpu
from jax.sharding import PartitionSpec as P

G = 4096
SUB = 64
UNROLL = 3
STACK = 4
LANES = 128
PITCH = 129
plane_step = 6.0
full_turn = 2.0 * math.pi
BF = ml_dtypes.bfloat16


def turn_poly():
    nodes = np.cos(np.pi * (np.arange(256) + 0.5) / 256)
    z = (nodes + 1.0) / 8.0
    f = np.sqrt(z)
    cos_c = np.polynomial.chebyshev.cheb2poly(
        np.polynomial.chebyshev.chebfit(nodes, np.cos(2 * np.pi * f), 5)
    )
    sin_c = np.polynomial.chebyshev.cheb2poly(
        np.polynomial.chebyshev.chebfit(nodes, np.sin(2 * np.pi * f) / f, 5)
    )
    base = np.polynomial.Polynomial([-1.0, 8.0])
    out = []
    for coefs in (cos_c, sin_c):
        total = np.polynomial.Polynomial([0.0])
        for c in coefs[::-1]:
            total = total * base + c
        out.append([float(c) for c in total.coef])
    return out


COS_C, SIN_C = turn_poly()


def cos_sin_turns(turns):
    f = turns - jnp.round(turns)
    z = f * f
    c = COS_C[-1] * z + COS_C[-2]
    for k in COS_C[-3::-1]:
        c = c * z + k
    s = SIN_C[-1] * z + SIN_C[-2]
    for k in SIN_C[-3::-1]:
        s = s * z + k
    return c, s * f


def half_orders():
    fine = np.arange(8) + 0.5
    return np.concatenate([fine, 16 - fine, 16 + fine, 32 - fine])


def dirichlet(x):
    bottom = np.sin(np.pi * x / SUB)
    zero = np.abs(bottom) < 1e-12
    return np.where(zero, float(SUB), np.sin(np.pi * x) / np.where(zero, 1.0, bottom))


def spread_table():
    at = (np.arange(G) - G // 2) / SUB + 0.5
    order = half_orders()[:, None]
    minus, plus = dirichlet(at[None] - order), dirichlet(at[None] + order)
    return np.concatenate([minus + plus, minus - plus], axis=0)


def column_table():
    return (spread_table() / SUB).astype(np.float32)


def row_table(parts):
    whole = (spread_table() / G).reshape(SUB, parts, SUB // parts, 64)
    return np.ascontiguousarray(whole.transpose(1, 3, 2, 0)).astype(BF)


def head_matrices():
    l0 = np.arange(64)[:, None]
    out = []
    for core in range(2):
        columns = []
        for source in range(2):
            t = (2 * np.arange(32) + (core ^ source))[None, :]
            ang = full_turn / 64 * np.mod(l0 * t, 64)
            c, s = np.cos(ang), np.sin(ang)
            columns.append(np.block([[c, -s], [s, c]]))
        out.append(np.concatenate(columns, axis=1))
    return np.stack(out).astype(BF)


def gather_kernel(far, near, x_ref, out_ref, z_send, z_recv, y_send, y_recv, c_send, c_recv):
    me = lax.axis_index("uv")
    c = lax.rem(me, 2)
    b = lax.rem(me // 2, near)
    a = me // (2 * near)

    def at(da, db, dc):
        return (
            lax.rem(a + da + far, far) * near + lax.rem(b + db + near, near)
        ) * 2 + lax.rem(c + dc, 2)

    peers = [at(d, 0, 0) for d in range(1, far)]
    peers += [at(0, e, 0) for e in range(1, near)] + [at(0, 0, 1)]
    barrier = pltpu.get_barrier_semaphore()
    for peer in peers:
        pl.semaphore_signal(
            barrier, inc=1, device_id={"uv": peer}, device_id_type=pl.DeviceIdType.MESH
        )
    pl.semaphore_wait(barrier, len(peers))

    def copy(source, slot, target, send, recv):
        return pltpu.make_async_remote_copy(
            src_ref=source,
            dst_ref=out_ref.at[slot],
            send_sem=send,
            recv_sem=recv,
            device_id={"uv": target},
            device_id_type=pl.DeviceIdType.MESH,
        )

    sent = []

    def send(source, slot, target, send_sem, recv_sem):
        one = copy(source, slot, target, send_sem, recv_sem)
        one.start()
        sent.append(one)

    for d in range(1, far):
        send(x_ref, me, at(d, 0, 0), z_send.at[d], z_recv.at[d])
    for d in range(far):
        slot = at(-d, 0, 0)
        source = x_ref if d == 0 else out_ref.at[slot]
        if d > 0:
            copy(x_ref, slot, me, z_send.at[d], z_recv.at[d]).wait_recv()
        for e in range(1, near):
            k = d * near + e
            send(source, slot, at(0, e, 0), y_send.at[k], y_recv.at[k])
        k = d * near
        send(source, slot, at(0, 0, 1), c_send.at[k], c_recv.at[k])
        if d == 0:
            out_ref[me] = x_ref[...]
    for d in range(far):
        for e in range(1, near):
            k = d * near + e
            slot = at(-d, -e, 0)
            copy(x_ref, slot, me, y_send.at[k], y_recv.at[k]).wait_recv()
            send(out_ref.at[slot], slot, at(0, 0, 1), c_send.at[k], c_recv.at[k])
    for d in range(far):
        for e in range(near):
            k = d * near + e
            copy(x_ref, at(-d, -e, 1), me, c_send.at[k], c_recv.at[k]).wait_recv()
    for one in sent:
        one.wait_send()


def gather_all(packed, uv_count):
    chips = uv_count // 2
    near = 1 << ((chips.bit_length() - 1) // 2)
    far = chips // near
    sems = [far] * 2 + [far * near] * 4
    return pl.pallas_call(
        functools.partial(gather_kernel, far, near),
        out_shape=jax.ShapeDtypeStruct((uv_count,) + packed.shape, packed.dtype),
        in_specs=[pl.BlockSpec(memory_space=pltpu.VMEM)],
        out_specs=pl.BlockSpec(memory_space=pltpu.VMEM),
        scratch_shapes=[pltpu.SemaphoreType.DMA((n,)) for n in sems],
        compiler_params=pltpu.CompilerParams(
            collective_id=0, has_side_effects=True, vmem_limit_bytes=24 * 1024 * 1024
        ),
    )(packed)


def grid_kernel(
    width, blocks, homes, data_ref, cols_ref, moff_ref, d_ref,
    keep_ref, give_ref, acc, rows_f, phase, slots, filled, group,
):
    devices = data_ref.shape[0]
    cap = 2 * devices
    half_tiles = G // SUB // 2
    k_len = data_ref.shape[2]
    acc[...] = jnp.zeros_like(acc)

    def empty(h, carry):
        filled[h] = 0
        return carry

    lax.fori_loop(0, half_tiles + 1, empty, 0)

    def spread(j, carry):
        rows_f[j] = data_ref[j].astype(jnp.float32)
        turn = jnp.bitwise_and((2 * cols_ref[j] - (G - SUB + 1)) * moff_ref[...], 2 * G - 1)
        pc, ps = cos_sin_turns(turn.astype(jnp.float32) * (0.5 / G))
        phase[j, 0] = pc
        phase[j, 1] = ps

        for i in range(blocks):
            h = homes[j * blocks + i]
            n = filled[h]
            slots[h * cap + n] = j * blocks + i
            filled[h] = n + 1
        return carry

    lax.fori_loop(0, devices, spread, 0)

    def list_groups(h, found):
        def one(g, n):
            group[3 * n] = h
            group[3 * n + 1] = h * cap + STACK * g
            group[3 * n + 2] = filled[h] - STACK * g
            return n + 1

        return lax.fori_loop(0, (filled[h] + STACK - 1) // STACK, one, found)

    total = lax.fori_loop(0, half_tiles, list_groups, 0)

    sub = lax.broadcasted_iota(jnp.int32, (8, k_len), 0)
    fine = (sub.astype(jnp.float32) + 0.5) * (1.0 / SUB)

    def pick(values):
        out = jnp.zeros((8, k_len), jnp.float32)
        for n, value in enumerate(values):
            if value:
                out = jnp.where(sub == n, value / SUB, out)
        return out

    coarse_u = pick((16.0, 32.0, 0.0, 0.0, -0.5))
    coarse_v = pick((0.0, 0.0, 16.0, 32.0, -0.5))
    scale = 1.0 / math.sqrt(k_len)

    def expand(c, s, c1, s1, c2, s2):
        a, b, d, e = c1 * c, s1 * s, s1 * c, c1 * s
        return (
            jnp.concatenate([c, a + b, a - b, c2 * c + s2 * s], axis=0),
            jnp.concatenate([s, d - e, d + e, s2 * c - c2 * s], axis=0),
        )

    def one_block(j, i, keep):
        vr, vi, u, v = (rows_f[j, pl.ds(q * blocks + i, 1), :] for q in range(4))
        u = u + 0.5
        v = v + 0.5
        cc, cs = cos_sin_turns(coarse_u * u + coarse_v * v)
        row = lambda n: (cc[n : n + 1], cs[n : n + 1])
        cu, su = expand(*cos_sin_turns(fine * u), *row(0), *row(1))
        cv, sv = expand(*cos_sin_turns(fine * v), *row(2), *row(3))
        hc, hs = row(4)
        wr = (vr * hc - vi * hs) * keep
        wi = (vr * hs + vi * hc) * keep
        left = jnp.concatenate([wr * cu, -wi * su, wi * cu, wr * su], axis=0)
        right = jnp.concatenate([cv, sv], axis=0)
        s = lax.dot_general(
            left.astype(jnp.bfloat16),
            right.astype(jnp.bfloat16),
            (((1,), (1,)), ((), ())),
            preferred_element_type=jnp.float32,
        ).astype(jnp.bfloat16)
        return s, phase[j, 0, pl.ds(i, 1), :], phase[j, 1, pl.ds(i, 1), :]

    def step(it, carry):
        for k in range(UNROLL):
            n = it * UNROLL + k
            real = n < total
            n = jnp.where(real, n, 0)
            h = group[3 * n]
            first = group[3 * n + 1]
            left_over = jnp.where(real, group[3 * n + 2], 0)
            made = []
            for q in range(STACK):
                live = q < left_over
                g = jnp.where(live, slots[first + q], 0)
                j = g // blocks
                made.append(one_block(j, g - j * blocks, jnp.where(live, scale, 0.0)))
            piece = jnp.concatenate([s for s, _, _ in made], axis=1)
            rows = pl.ds(h * PITCH, 2 * SUB)
            half = 2 * width
            for lane in range(0, half, min(half, 256)):
                cut = slice(lane, lane + min(half, 256))
                dc, ds = d_ref[:32, cut], d_ref[32:, cut]
                for turn in range(2):
                    weight = []
                    for _, pr, pi in made:
                        pr, pi = pr[:, cut], pi[:, cut]
                        weight += [dc * pi, ds * pr] if turn else [dc * pr, ds * -pi]
                    got = jnp.dot(
                        piece,
                        jnp.concatenate(weight, axis=0).astype(jnp.bfloat16),
                        preferred_element_type=jnp.float32,
                    )
                    for c in range(got.shape[1] // LANES):
                        at = (turn * half + lane) // LANES + c
                        acc[at, rows, :] += got[:, c * LANES : (c + 1) * LANES]
        return carry

    lax.fori_loop(0, (total + UNROLL - 1) // UNROLL, step, 0)

    def turned(lam, carry):
        chunks = 2 * width // LANES
        top = [acc[c, pl.ds(lam, half_tiles, stride=PITCH), :] for c in range(2 * chunks)]
        low = [acc[c, pl.ds(SUB + lam, half_tiles, stride=PITCH), :] for c in range(2 * chunks)]
        re = jnp.concatenate([top[c] - low[chunks + c] for c in range(chunks)], axis=1)
        im = jnp.concatenate([top[chunks + c] + low[c] for c in range(chunks)], axis=1)
        keep_ref[lam] = jnp.concatenate([re[:, :width], im[:, :width]], axis=0).astype(jnp.bfloat16)
        give_ref[lam] = jnp.concatenate([re[:, width:], im[:, width:]], axis=0).astype(jnp.bfloat16)
        return carry

    lax.fori_loop(0, SUB, turned, 0, unroll=4)


def in_lanes(rows):
    width = rows.shape[1]
    if width < LANES:
        return [jnp.concatenate([rows] * (LANES // width), axis=1)]
    return [rows[:, c : c + LANES] for c in range(0, width, LANES)]


def lane_chunks(width):
    return max(1, width // LANES)


def tail_rows(width, share, place, y_of, table, out_t):
    part, depth, m_first = place

    def step(l0, carry):
        z = jnp.dot(table[l0], y_of(l0), preferred_element_type=jnp.float32)
        l1 = part * share + lax.broadcasted_iota(jnp.int32, (share, width), 0)
        l = l0 + 64 * l1 - G // 2
        m = m_first + lax.broadcasted_iota(jnp.int32, (share, width), 1)
        x = l.astype(jnp.float32) * (1.0 / G)
        y = m.astype(jnp.float32) * (1.0 / G)
        ramp = jnp.bitwise_and(-(G - SUB + 1) * l, 2 * G - 1).astype(jnp.float32) * (0.5 / G)
        sc, ss = cos_sin_turns(depth * (jnp.sqrt(1.0 - y * y - x * x) - 1.0) + ramp)
        for c, rows in enumerate(in_lanes(z[:, :width] * sc - z[:, width:] * ss)):
            out_t[c, pl.ds(l0, share, stride=64), :] = rows
        return carry

    lax.fori_loop(0, 64, step, 0, unroll=4)


def turn_out(out_t, out_ref):
    chunk = 128

    def step(n, carry):
        at = pl.multiple_of(n * chunk, chunk)
        for c in range(out_t.shape[0]):
            turned = out_t[c, pl.ds(at, chunk), :].T.astype(out_ref.dtype)
            width = min(LANES, out_ref.shape[0])
            out_ref[c * width : (c + 1) * width, pl.ds(at, chunk)] = turned[:width]
        return carry

    lax.fori_loop(0, out_t.shape[1] // chunk, step, 0, unroll=4)


def head_kernel(
    width, share, places, depths, own_ref, came_ref, head_ref, table, y_ref, out_ref, mid, out_t
):
    def head(lam, carry):
        rhs = jnp.concatenate([own_ref[lam], came_ref[lam]], axis=0)
        got = jnp.dot(head_ref[...], rhs, preferred_element_type=jnp.float32)
        for c, rows in enumerate(in_lanes(got)):
            mid[c, pl.ds(lam * PITCH, 128), :] = rows
        return carry

    lax.fori_loop(0, SUB, head, 0, unroll=4)

    def y_of(l0):
        halves = []
        for first in (0, 64):
            rows = [mid[c, pl.ds(first + l0, SUB, stride=PITCH), :] for c in range(mid.shape[0])]
            halves += [r[:, : min(width, LANES)] for r in rows]
        y = jnp.concatenate(halves, axis=1).astype(jnp.bfloat16)
        y_ref[l0] = y
        return y

    tail_rows(width, share, (places[0], depths[0], places[1]), y_of, table, out_t)
    turn_out(out_t, out_ref)


def tail_kernel(width, share, places, depths, y_ref, table, out_ref, out_t):
    tail_rows(
        width, share, (places[0], depths[0], places[1]), lambda l0: y_ref[l0], table, out_t
    )
    turn_out(out_t, out_ref)


def on_device(visibility, coords, tile_row, col_offset, live_count):
    uv_count = lax.axis_size("uv")
    wa_count = lax.axis_size("wa")
    uv_index = lax.axis_index("uv")
    wa_index = lax.axis_index("wa")
    blocks = visibility.shape[0]
    k_len = visibility.shape[2]
    width = G // uv_count
    core = jnp.mod(uv_index, 2)
    partner = uv_index + 1 - 2 * core
    numbers = jnp.stack(
        [
            tile_row[:, 0],
            col_offset // SUB,
            jnp.mod(col_offset, SUB),
            jnp.broadcast_to(live_count[0], (blocks,)),
        ]
    )
    numbers = jnp.pad(numbers, ((0, 12), (0, k_len - blocks))).astype(jnp.bfloat16)
    packed = jnp.concatenate(
        [visibility[:, 0], visibility[:, 1], coords[:, 0], coords[:, 1], numbers], axis=0
    )
    columns = jnp.asarray(column_table())
    d_table = jnp.concatenate(
        [
            lax.dynamic_slice_in_dim(columns, uv_index * width, width, 1),
            lax.dynamic_slice_in_dim(columns, partner * width, width, 1),
        ],
        axis=1,
    )
    m_first = uv_index * width - G // 2
    m_both = jnp.concatenate(
        [m_first + jnp.arange(width), partner * width + jnp.arange(width) - G // 2]
    )[None, :]
    all_data = gather_all(packed, uv_count)
    came_numbers = all_data[:, 4 * blocks : 4 * blocks + 4, :blocks].astype(jnp.int32)
    tiles = came_numbers[:, 0]
    live = jnp.arange(blocks)[None, :] < came_numbers[:, 3]
    mine = live & (jnp.mod(tiles, 2) == core)
    homes = jnp.where(mine, tiles // 2, G // SUB // 2).reshape(-1)
    cols = (came_numbers[:, 1] * SUB + came_numbers[:, 2])[:, :, None]

    rows = packed.shape[0]
    half_tiles = G // SUB // 2
    cap = 2 * uv_count
    shape = (SUB, SUB, width)
    vmem = pl.BlockSpec(memory_space=pltpu.VMEM)
    smem = pl.BlockSpec(memory_space=pltpu.SMEM)
    own, give = pl.pallas_call(
        functools.partial(grid_kernel, width, blocks),
        out_shape=[jax.ShapeDtypeStruct(shape, jnp.bfloat16)] * 2,
        in_specs=[smem, vmem, vmem, vmem, vmem],
        out_specs=[vmem, vmem],
        scratch_shapes=[
            pltpu.VMEM((4 * width // LANES, half_tiles * PITCH, LANES), jnp.float32),
            pltpu.VMEM((uv_count, rows, k_len), jnp.float32),
            pltpu.VMEM((uv_count, 2, blocks, 2 * width), jnp.float32),
            pltpu.SMEM((half_tiles * cap + uv_count * blocks,), jnp.int32),
            pltpu.SMEM((half_tiles + 1,), jnp.int32),
            pltpu.SMEM((3 * (uv_count * blocks // STACK + half_tiles),), jnp.int32),
        ],
        compiler_params=pltpu.CompilerParams(vmem_limit_bytes=48 * 1024 * 1024),
    )(homes, all_data, cols, m_both, d_table)
    came_half = lax.ppermute(give, "uv", [(n, n ^ 1) for n in range(uv_count)])

    share = 64 // wa_count
    depth = ((wa_index.astype(jnp.float32) - (wa_count - 1) / 2.0) * plane_step)[None]
    tables = jnp.asarray(row_table(wa_count))
    span = G // wa_count

    def places_of(part):
        return jnp.stack([part, m_first]).astype(jnp.int32)

    def head_of(part, dtype):
        return pl.pallas_call(
            functools.partial(head_kernel, width, share),
            out_shape=[
                jax.ShapeDtypeStruct((64, SUB, 2 * width), jnp.bfloat16),
                jax.ShapeDtypeStruct((width, span), dtype),
            ],
            in_specs=[smem, smem, vmem, vmem, vmem, vmem],
            out_specs=[vmem, vmem],
            scratch_shapes=[
                pltpu.VMEM((lane_chunks(width), SUB * PITCH, LANES), jnp.float32),
                pltpu.VMEM((lane_chunks(width), span, LANES), jnp.float32),
            ],
            compiler_params=pltpu.CompilerParams(vmem_limit_bytes=40 * 1024 * 1024),
        )(
            places_of(part), depth, own, came_half, jnp.asarray(head_matrices())[core], tables[part]
        )

    def tail_of(part, first, dtype):
        return pl.pallas_call(
            functools.partial(tail_kernel, width, share),
            out_shape=jax.ShapeDtypeStruct((width, span), dtype),
            in_specs=[smem, smem, vmem, vmem],
            out_specs=vmem,
            scratch_shapes=[pltpu.VMEM((lane_chunks(width), span, LANES), jnp.float32)],
            compiler_params=pltpu.CompilerParams(vmem_limit_bytes=40 * 1024 * 1024),
        )(places_of(part), depth, first, tables[part])

    if wa_count == 2:
        first, away = head_of(1 - wa_index, jnp.bfloat16)
        came = lax.ppermute(away, "wa", [(0, 1), (1, 0)])
        return tail_of(wa_index, first, jnp.float32) + came.astype(jnp.float32)
    first, part = head_of(jnp.int32(0), jnp.bfloat16)
    images = [part] + [tail_of(jnp.int32(n), first, jnp.bfloat16) for n in range(1, wa_count)]
    parts = jnp.stack(images, axis=1)
    came = lax.all_to_all(parts, "wa", split_axis=1, concat_axis=1)
    return jnp.sum(came.astype(jnp.float32), axis=1)


def solution(mesh):
    in_specs = (
        P(("wa", "uv"), None, None),
        P(("wa", "uv"), None, None),
        P(("wa", "uv"), None),
        P(("wa", "uv")),
        P("wa", "uv"),
    )
    return jax.shard_map(
        on_device, mesh=mesh, in_specs=in_specs, out_specs=P("uv", "wa"), check_vma=False
    )
```

time: 137 us -> 113 us (0.82)
  local copies, waits for them, and re-layouts: 13.3 us -> 4.8 us
  other arithmetic: 9.37 us -> 3.26 us
  matrix products: 5.42 us -> 0 us
  waiting for transfers between devices: 24.1 us -> 21.3 us
    pallas_call x0 -> x2, Pallas kernels: none -> 17.7 us  [the longest x1 11.1 us: head_of(): pl.pallas_call(functools.partial(head_kernel, width, share), out_shape=[j...]
    pallas_call x1, Pallas kernels: 60.9 us -> 43.5 us  [on_device(): pl.pallas_call(functools.partial(grid_kernel, width, blocks), out_shape=[...]
    transpose x2 -> x0, other arithmetic: 6.85 us -> none  [in_order(): return screened.transpose(1, 2, 0).reshape(width, G // wa_count)]
    dot_general x5 -> x0, matrix products: 5.42 us -> none  [the longest x2 2.73 us: on_device(): jnp.dot(jnp.asarray(np.block([[fr.T, -fi.T], [fi.T, fr.T]]) / SUB), jnp.c...]
    unnamed x23 -> x12, local copies, waits for them, and re-layouts: 6.49 us -> 1.38 us
    ppermute x1, waiting for transfers between devices: 20.2 us -> 17 us  [on_device(): came = lax.ppermute(away, 'wa', [(0, 1), (1, 0)])]
    transpose x4 -> x0, local copies, waits for them, and re-layouts: 2.96 us -> none  [the longest x2 1.81 us: in_order(): return screened.transpose(1, 2, 0).reshape(width, G // wa_count)]
    concatenate x3 -> x2, other arithmetic: 2.07 us -> 0.02 us  [the longest x1 0.01 us: on_device(): jnp.concatenate([lax.dynamic_slice_in_dim(columns, uv_index * width, widt...]
  transfers between devices with their start and end apart: 2 -> 2, of which waited for: 2 -> 2; matrix products, arithmetic and copies ran while one was open for 4% -> 0% of each run, Pallas kernels for 0% -> 6%
where the time goes in v1:
time: 113 us; the launch traced here: 114 us
  Pallas kernels  82 us (73%)
  waiting for transfers between devices  21.3 us (19%)
  local copies, waits for them, and re-layouts  4.8 us (4%)
  other arithmetic  3.26 us (3%)
  starting transfers between devices  1.57 us (1%)
    pallas_call x1, Pallas kernels, on_device(): pl.pallas_call(functools.partial(grid_kernel, width, blocks), out_shape=[...  43.5 us
    pallas_call x1, Pallas kernels, gather_all(): pl.pallas_call(functools.partial(gather_kernel, far, near), out_shape=jax...  20.8 us
    ppermute x1, waiting for transfers between devices, on_device(): came = lax.ppermute(away, 'wa', [(0, 1), (1, 0)])  17 us
    pallas_call x1, Pallas kernels, head_of(): pl.pallas_call(functools.partial(head_kernel, width, share), out_shape=[j...  11.1 us
    pallas_call x1, Pallas kernels, tail_of(): pl.pallas_call(functools.partial(tail_kernel, width, share), out_shape=ja...  6.6 us
    ppermute x1, waiting for transfers between devices, on_device(): came_half = lax.ppermute(give, 'uv', [(n, n ^ 1) for n in range(uv_count)])  4.33 us
  transfers between devices with their start and end apart: 2, of which 2 were waited for; matrix products, arithmetic and copies ran while one was open for 0% of the time, Pallas kernels for 6%

profile of v1, /device:TPU:0, one launch (start us, length us, event | category | flops | bytes accessed | tf_op | source)
XLA Modules:
  0.0 113.7 jit_solution(1325566321968146842)
XLA Ops:
  0.7 0.7 convert_bitcast_fusion.1
  1.3 0.7 convert_bitcast_fusion
  2.0 0.1 lt.45
  2.1 1.0 fusion.12
  3.0 1.0 fusion.11
  4.0 0.1 pad.13.clone
  4.1 0.1 maximum_maximum_fusion
  4.2 20.8 %shard_map.82.data_ref = bf16[16,208,256]{2,1,0:T(8,128)(2,1)S(1)} custom-call(bf16[208,256]{1,0:T(8,128)(2,1)S(1)} %constant_dynamic-update-slice_fusion.x_ref), custom_call_target="tpu_custom_call" | custom-call | tf_op jit(solution)/shard_map/pallas_call | solution.py:170
  25.0 0.0 copy-start.3
  25.0 0.0 copy-start.2
  25.0 0.1 slice_reduce_fusion.1
  25.1 0.1 squeeze.37
  25.2 0.1 squeeze.38
  25.2 0.2 copy.18.cols_ref
  25.5 0.9 constant_dynamic-slice_fusion.1
  26.4 43.5 %shard_map.83 = (bf16[64,64,256]{2,1,0:T(8,128)(2,1)S(1)}, bf16[64,64,256]{2,1,0:T(8,128)(2,1)}) custom-call(s32[768]{0:T(1024)S(1)} %fusion.5.homes, bf16[16,208,256]{2,1,0:T(8,128)(2,1)S(1)} %shard_map.82.data_ref, s32[16,48,1]{2,1,0:T(8,128)S(1)} %copy.18.cols_ref, s32[1,512]{1,0:T(1,128)S(1)} %bitcast.37, f32[64,512]{1,0:T(8,128)S(1)} %pad_maximum_fusion.d_ref), custom_call_target="tpu_custom_call" | custom-call | tf_op jit(solution)/shard_map/pallas_call | solution.py:441
  69.9 0.0 copy-start
  69.9 1.3 %copy-done = bf16[64,64,256]{2,1,0:T(8,128)(2,1)} copy-done((bf16[64,64,256]{2,1,0:T(8,128)(2,1)}, bf16[64,64,256]{2,1,0:T(8,128)(2,1)S(1)}, u32[]{:S(2)}) %copy-start) | copy-done | bytes 2097176
  71.2 0.0 copy-start.1
  71.2 0.0 collective-permute-start
  71.2 0.1 pad_add_fusion.2.places
  71.3 0.0 copy-done.3
  71.3 0.0 copy-done.2
  71.3 0.1 dynamic-slice_bitcast_fusion
  71.4 4.3 %collective-permute-done.came_ref = bf16[64,64,256]{2,1,0:T(8,128)(2,1)} collective-permute-done((bf16[64,64,256]{2,1,0:T(8,128)(2,1)}, bf16[64,64,256]{2,1,0:T(8,128)(2,1)}, u32[]{:S(2)}, u32[]{:S(2)}) %collective-permute-start) | collective-permute-done | bytes 2097184 | tf_op jit(solution)/shard_map/ppermute | solution.py:456
  75.7 0.0 copy-done.1
  75.7 11.1 %shard_map.84 = (bf16[64,64,512]{2,1,0:T(8,128)(2,1)S(1)}, bf16[256,2048]{1,0:T(8,128)(2,1)S(1)}) custom-call(s32[2]{0:T(128)S(1)} %pad_add_fusion.2.places, f32[1]{0:T(128)} %bitcast.2.depths, bf16[64,64,256]{2,1,0:T(8,128)(2,1)S(1)} %copy-done.1, bf16[64,64,256]{2,1,0:T(8,128)(2,1)} %collective-permute-done.came_ref, ...), custom_call_target="tpu_custom_call" | custom-call | tf_op jit(solution)/shard_map/pallas_call | solution.py:467
  86.9 1.6 %collective-permute-start.1 = (bf16[256,2048]{1,0:T(8,128)(2,1)S(1)}, bf16[256,2048]{1,0:T(8,128)(2,1)S(1)}, u32[]{:S(2)}, u32[]{:S(2)}) collective-permute-start(bf16[256,2048]{1,0:T(8,128)(2,1)S(1)} %get-tuple-element.12), channel_id=1, source_target_pairs={{0,16},{16,0},{1,17},{17,1},{2,18},{18,2},{3,19},{19,3},{4,20},{20... | collective-permute-start | bytes 3145736 | tf_op jit(solution)/shard_map/ppermute | solution.py:496
  88.4 0.1 pad_add_fusion.1.places
  88.5 6.6 %shard_map.85 = f32[256,2048]{1,0:T(8,128)S(1)} custom-call(s32[2]{0:T(128)S(1)} %pad_add_fusion.1.places, f32[1]{0:T(128)} %bitcast.2.depths, bf16[64,64,512]{2,1,0:T(8,128)(2,1)S(1)} %get-tuple-element.11.y_ref, bf16[64,32,64]{2,1,0:T(8,128)(2,1)S(1)} %get-tuple-element.15.table), custom_call_target="tpu_custom_call" | custom-call | tf_op jit(solution)/shard_map/pallas_call | solution.py:485
  95.1 17.0 %collective-permute-done.1 = bf16[256,2048]{1,0:T(8,128)(2,1)S(1)} collective-permute-done((bf16[256,2048]{1,0:T(8,128)(2,1)S(1)}, bf16[256,2048]{1,0:T(8,128)(2,1)S(1)}, u32[]{:S(2)}, u32[]{:S(2)}) %collective-permute-start.1) | collective-permute-done | bytes 1048608 | tf_op jit(solution)/shard_map/ppermute | solution.py:496
  112.1 1.6 %convert_add_fusion = f32[256,2048]{1,0:T(8,128)} fusion(f32[256,2048]{1,0:T(8,128)S(1)} %shard_map.85, bf16[256,2048]{1,0:T(8,128)(2,1)S(1)} %collective-permute-done.1), kind=kLoop, calls=%fused_computation | loop fusion | flops 1048576 | bytes 5242880 | tf_op jit(solution)/shard_map/add | solution.py:497
  (12 shorter events, 0.1 us)
Async XLA Ops:
  25.0 46.3 %copy-start.3 = (bf16[2,128,128]{2,1,0:T(8,128)(2,1)S(1)}, bf16[2,128,128]{2,1,0:T(8,128)(2,1)}, u32[]{:S(2)}) copy-start(bf16[2,128,128]{2,1,0:T(8,128)(2,1)} %constant.97.clone) | copy-start | bytes 196612
  25.0 46.3 %copy-start.2 = (bf16[2,64,32,64]{3,2,1,0:T(8,128)(2,1)S(1)}, bf16[2,64,32,64]{3,2,1,0:T(8,128)(2,1)}, u32[]{:S(2)}) copy-start(bf16[2,64,32,64]{3,2,1,0:T(8,128)(2,1)} %constant.96.clone) | copy-start | bytes 1572868
  69.9 1.3 %copy-start = (bf16[64,64,256]{2,1,0:T(8,128)(2,1)}, bf16[64,64,256]{2,1,0:T(8,128)(2,1)S(1)}, u32[]{:S(2)}) copy-start(bf16[64,64,256]{2,1,0:T(8,128)(2,1)S(1)} %get-tuple-element.9.own_ref) | copy-start | bytes 6291460
  71.2 4.5 %copy-start.1 = (bf16[64,64,256]{2,1,0:T(8,128)(2,1)S(1)}, bf16[64,64,256]{2,1,0:T(8,128)(2,1)}, u32[]{:S(2)}) copy-start(bf16[64,64,256]{2,1,0:T(8,128)(2,1)} %copy-done) | copy-start | bytes 6291460
  71.2 4.5 %collective-permute-start = (bf16[64,64,256]{2,1,0:T(8,128)(2,1)}, bf16[64,64,256]{2,1,0:T(8,128)(2,1)}, u32[]{:S(2)}, u32[]{:S(2)}) collective-permute-start(bf16[64,64,256]{2,1,0:T(8,128)(2,1)} %get-tuple-element.10), channel_id=1, source_target_pairs={{0,1},{1,0},{2,3},{3,2},{4,5},{5,4},{6,7},{7,6},{8,9},{9,8},{10,11... | collective-permute-start | bytes 6291464 | tf_op jit(solution)/shard_map/ppermute | solution.py:456
  86.9 25.3 %collective-permute-start.1 = (bf16[256,2048]{1,0:T(8,128)(2,1)S(1)}, bf16[256,2048]{1,0:T(8,128)(2,1)S(1)}, u32[]{:S(2)}, u32[]{:S(2)}) collective-permute-start(bf16[256,2048]{1,0:T(8,128)(2,1)S(1)} %get-tuple-element.12), channel_id=1, source_target_pairs={{0,16},{16,0},{1,17},{17,1},{2,18},{18,2},{3,19},{19,3},{4,20},{20... | collective-permute-start | bytes 3145736 | tf_op jit(solution)/shard_map/ppermute | solution.py:496

commit v2 on v1

--- a/solution.py
+++ b/solution.py
@@ -12,26 +12,29 @@
 
 G = 4096
 SUB = 64
-UNROLL = 3
+BATCH = 8
 STACK = 4
 LANES = 128
 PITCH = 129
+OUT_PITCH = 65
+SWAPS = 2
+SENDS = 4
 plane_step = 6.0
 full_turn = 2.0 * math.pi
 BF = ml_dtypes.bfloat16
 
 
-def turn_poly():
+def turn_poly(bound, degree):
     nodes = np.cos(np.pi * (np.arange(256) + 0.5) / 256)
-    z = (nodes + 1.0) / 8.0
+    z = (nodes + 1.0) / (2.0 * bound)
     f = np.sqrt(z)
     cos_c = np.polynomial.chebyshev.cheb2poly(
-        np.polynomial.chebyshev.chebfit(nodes, np.cos(2 * np.pi * f), 5)
+        np.polynomial.chebyshev.chebfit(nodes, np.cos(2 * np.pi * f), degree)
     )
     sin_c = np.polynomial.chebyshev.cheb2poly(
-        np.polynomial.chebyshev.chebfit(nodes, np.sin(2 * np.pi * f) / f, 5)
+        np.polynomial.chebyshev.chebfit(nodes, np.sin(2 * np.pi * f) / f, degree)
     )
-    base = np.polynomial.Polynomial([-1.0, 8.0])
+    base = np.polynomial.Polynomial([-1.0, 2.0 * bound])
     out = []
     for coefs in (cos_c, sin_c):
         total = np.polynomial.Polynomial([0.0])
@@ -41,19 +44,32 @@
     return out
 
 
-COS_C, SIN_C = turn_poly()
-
-
-def cos_sin_turns(turns):
-    f = turns - jnp.round(turns)
+COS_C, SIN_C = turn_poly(4.0, 5)
+COS_S, SIN_S = turn_poly(16.0, 4)
+
+
+def cos_sin_part(f, cos_c, sin_c):
     z = f * f
-    c = COS_C[-1] * z + COS_C[-2]
-    for k in COS_C[-3::-1]:
+    c = cos_c[-1] * z + cos_c[-2]
+    for k in cos_c[-3::-1]:
         c = c * z + k
-    s = SIN_C[-1] * z + SIN_C[-2]
-    for k in SIN_C[-3::-1]:
+    s = sin_c[-1] * z + sin_c[-2]
+    for k in sin_c[-3::-1]:
         s = s * z + k
     return c, s * f
+
+
+def cos_sin_turns(turns):
+    return cos_sin_part(turns - jnp.round(turns), COS_C, SIN_C)
+
+
+def times(a, b):
+    return a[0] * b[0] - a[1] * b[1], a[0] * b[1] + a[1] * b[0]
+
+
+def squared(a):
+    twice = a[0] + a[0]
+    return twice * a[0] - 1.0, twice * a[1]
 
 
 def half_orders():
@@ -74,8 +90,9 @@
     return np.concatenate([minus + plus, minus - plus], axis=0)
 
 
-def column_table():
-    return (spread_table() / SUB).astype(np.float32)
+def column_table(devices):
+    whole = (spread_table() / SUB).reshape(SUB, devices, G // devices)
+    return np.ascontiguousarray(whole.transpose(1, 0, 2)).astype(np.float32)
 
 
 def row_table(parts):
@@ -180,32 +197,45 @@
 
 
 def grid_kernel(
-    width, blocks, homes, data_ref, cols_ref, moff_ref, d_ref,
-    keep_ref, give_ref, acc, rows_f, phase, slots, filled, group,
+    width, blocks, k_len, homes, data_ref, cols_ref, m_ref, d_all, keep_ref, give_ref,
+    acc, rows_f, slots, filled, group, d_ref, *buffers,
 ):
     devices = data_ref.shape[0]
     cap = 2 * devices
     half_tiles = G // SUB // 2
-    k_len = data_ref.shape[2]
-    acc[...] = jnp.zeros_like(acc)
+    both = 2 * width
+    k_parts = k_len // LANES
+    m_parts = both // LANES
+    each = 5 * blocks
+    uv = lax.axis_index("uv")
+    stage = buffers[0]
+    sets = (buffers[1:5], buffers[5:9])
+    d_ref[:, :width] = d_all[uv]
+    d_ref[:, width:] = d_all[uv + 1 - 2 * lax.rem(uv, 2)]
 
     def empty(h, carry):
         filled[h] = 0
         return carry
 
     lax.fori_loop(0, half_tiles + 1, empty, 0)
+    clear = max(1, half_tiles // devices) * PITCH
 
     def spread(j, carry):
-        rows_f[j] = data_ref[j].astype(jnp.float32)
-        turn = jnp.bitwise_and((2 * cols_ref[j] - (G - SUB + 1)) * moff_ref[...], 2 * G - 1)
-        pc, ps = cos_sin_turns(turn.astype(jnp.float32) * (0.5 / G))
-        phase[j, 0] = pc
-        phase[j, 1] = ps
-
+        at = jnp.minimum(j * clear, half_tiles * PITCH - clear)
+        for c in range(2 * m_parts):
+            acc[c, pl.ds(at, clear), :] = jnp.zeros((clear, LANES), jnp.float32)
+        base = pl.multiple_of(j * each, 8)
+        for c in range(k_parts):
+            rows_f[c, pl.ds(base, 4 * blocks), :] = data_ref[
+                j, : 4 * blocks, c * LANES : (c + 1) * LANES
+            ].astype(jnp.float32)
+        rows_f[0, pl.ds(base + 4 * blocks, blocks), :] = jnp.broadcast_to(
+            cols_ref[j], (blocks, LANES)
+        )
         for i in range(blocks):
             h = homes[j * blocks + i]
             n = filled[h]
-            slots[h * cap + n] = j * blocks + i
+            slots[h * cap + n] = j * each + i
             filled[h] = n + 1
         return carry
 
@@ -221,20 +251,56 @@
         return lax.fori_loop(0, (filled[h] + STACK - 1) // STACK, one, found)
 
     total = lax.fori_loop(0, half_tiles, list_groups, 0)
-
-    sub = lax.broadcasted_iota(jnp.int32, (8, k_len), 0)
-    fine = (sub.astype(jnp.float32) + 0.5) * (1.0 / SUB)
-
-    def pick(values):
-        out = jnp.zeros((8, k_len), jnp.float32)
-        for n, value in enumerate(values):
-            if value:
-                out = jnp.where(sub == n, value / SUB, out)
-        return out
-
-    coarse_u = pick((16.0, 32.0, 0.0, 0.0, -0.5))
-    coarse_v = pick((0.0, 0.0, 16.0, 32.0, -0.5))
     scale = 1.0 / math.sqrt(k_len)
+
+    def prepare(batch, refs):
+        fine, coarse, signal, phase = refs
+        for p in range(BATCH // STACK):
+            n = batch * (BATCH // STACK) + p
+            real = n < total
+            n = jnp.where(real, n, 0)
+            first = group[3 * n + 1]
+            left_over = jnp.where(real, group[3 * n + 2], 0)
+            for q in range(STACK):
+                live = q < left_over
+                row = jnp.where(live, slots[first + q], 0)
+                keep = jnp.where(live, scale, 0.0)
+                k = p * STACK + q
+                for c in range(k_parts):
+                    for r in range(4):
+                        value = rows_f[c, pl.ds(row + r * blocks, 1), :]
+                        stage[r, c, k : k + 1, :] = value * keep if r < 2 else value
+                stage[4, 0, k : k + 1, :] = rows_f[0, pl.ds(row + 4 * blocks, 1), :]
+        for c in range(k_parts):
+            halves = []
+            for axis in range(2):
+                turns = (stage[2 + axis, c] + 0.5) * (0.5 / SUB)
+                half = cos_sin_part(turns, COS_S, SIN_S)
+                halves.append(half)
+                step = squared(half)
+                power = half
+                for b in range(8):
+                    if b:
+                        power = times(power, step)
+                    for e in range(2):
+                        fine[axis, e, c, b * 9 : b * 9 + 8, :] = power[e]
+                power = squared(times(power, half))
+                for e in range(2):
+                    coarse[4 * axis + e, c] = power[e]
+                power = squared(power)
+                for e in range(2):
+                    coarse[4 * axis + 2 + e, c] = power[e]
+            hc, hs = times(*halves)
+            vr, vi = stage[0, c], stage[1, c]
+            signal[0, c] = vr * hc + vi * hs
+            wi = vi * hc - vr * hs
+            signal[1, c] = wi
+            signal[2, c] = -wi
+        for c in range(m_parts):
+            pc, ps = cos_sin_turns(stage[4, 0] * m_ref[:, c * LANES : (c + 1) * LANES])
+            phase[0, c] = pc
+            phase[1, c] = ps
+            phase[2, c] = -ps
 
     def expand(c, s, c1, s1, c2, s2):
         a, b, d, e = c1 * c, s1 * s, s1 * c, c1 * s
@@ -243,72 +309,81 @@
             jnp.concatenate([s, d - e, d + e, s2 * c - c2 * s], axis=0),
         )
 
-    def one_block(j, i, keep):
-        vr, vi, u, v = (rows_f[j, pl.ds(q * blocks + i, 1), :] for q in range(4))
-        u = u + 0.5
-        v = v + 0.5
-        cc, cs = cos_sin_turns(coarse_u * u + coarse_v * v)
-        row = lambda n: (cc[n : n + 1], cs[n : n + 1])
-        cu, su = expand(*cos_sin_turns(fine * u), *row(0), *row(1))
-        cv, sv = expand(*cos_sin_turns(fine * v), *row(2), *row(3))
-        hc, hs = row(4)
-        wr = (vr * hc - vi * hs) * keep
-        wi = (vr * hs + vi * hc) * keep
-        left = jnp.concatenate([wr * cu, -wi * su, wi * cu, wr * su], axis=0)
-        right = jnp.concatenate([cv, sv], axis=0)
-        s = lax.dot_general(
-            left.astype(jnp.bfloat16),
-            right.astype(jnp.bfloat16),
+    def piece_of(k, refs):
+        fine, coarse, signal, _ = refs
+        lefts, rights = [], []
+        for c in range(k_parts):
+            tables = []
+            for axis in range(2):
+                start = [fine[axis, e, c, pl.ds(k, 8, stride=9), :] for e in range(2)]
+                rows = [coarse[4 * axis + n, c, k : k + 1, :] for n in range(4)]
+                tables.append(expand(*start, *rows))
+            (cu, su), (cv, sv) = tables
+            wr, wi, nwi = (signal[n, c, k : k + 1, :] for n in range(3))
+            lefts.append(
+                jnp.concatenate([wr * cu, nwi * su, wi * cu, wr * su], axis=0).astype(jnp.bfloat16)
+            )
+            rights.append(jnp.concatenate([cv, sv], axis=0).astype(jnp.bfloat16))
+        return lax.dot_general(
+            jnp.concatenate(lefts, axis=1),
+            jnp.concatenate(rights, axis=1),
             (((1,), (1,)), ((), ())),
             preferred_element_type=jnp.float32,
         ).astype(jnp.bfloat16)
-        return s, phase[j, 0, pl.ds(i, 1), :], phase[j, 1, pl.ds(i, 1), :]
-
-    def step(it, carry):
-        for k in range(UNROLL):
-            n = it * UNROLL + k
-            real = n < total
-            n = jnp.where(real, n, 0)
-            h = group[3 * n]
-            first = group[3 * n + 1]
-            left_over = jnp.where(real, group[3 * n + 2], 0)
-            made = []
-            for q in range(STACK):
-                live = q < left_over
-                g = jnp.where(live, slots[first + q], 0)
-                j = g // blocks
-                made.append(one_block(j, g - j * blocks, jnp.where(live, scale, 0.0)))
-            piece = jnp.concatenate([s for s, _, _ in made], axis=1)
+
+    def gather_up(batch, refs):
+        phase = refs[3]
+        for p in range(BATCH // STACK):
+            n = batch * (BATCH // STACK) + p
+            h = group[3 * jnp.where(n < total, n, 0)]
             rows = pl.ds(h * PITCH, 2 * SUB)
-            half = 2 * width
-            for lane in range(0, half, min(half, 256)):
-                cut = slice(lane, lane + min(half, 256))
-                dc, ds = d_ref[:32, cut], d_ref[32:, cut]
+            ks = range(p * STACK, (p + 1) * STACK)
+            piece = jnp.concatenate([piece_of(k, refs) for k in ks], axis=1)
+            wide = min(2, m_parts)
+            for c0 in range(0, m_parts, wide):
                 for turn in range(2):
                     weight = []
-                    for _, pr, pi in made:
-                        pr, pi = pr[:, cut], pi[:, cut]
-                        weight += [dc * pi, ds * pr] if turn else [dc * pr, ds * -pi]
+                    for k in ks:
+                        top, low = [], []
+                        for c in range(c0, c0 + wide):
+                            cut = slice(c * LANES, (c + 1) * LANES)
+                            pr, pi, npi = (phase[e, c, k : k + 1, :] for e in range(3))
+                            top.append(d_ref[:32, cut] * (pi if turn else pr))
+                            low.append(d_ref[32:, cut] * (pr if turn else npi))
+                        weight += [jnp.concatenate(top, axis=1), jnp.concatenate(low, axis=1)]
                     got = jnp.dot(
                         piece,
                         jnp.concatenate(weight, axis=0).astype(jnp.bfloat16),
                         preferred_element_type=jnp.float32,
                     )
-                    for c in range(got.shape[1] // LANES):
-                        at = (turn * half + lane) // LANES + c
+                    for c in range(wide):
+                        at = turn * m_parts + c0 + c
                         acc[at, rows, :] += got[:, c * LANES : (c + 1) * LANES]
+
+    batches = (total + BATCH // STACK - 1) // (BATCH // STACK)
+    prepare(0, sets[0])
+
+    def step(it, carry):
+        for n in range(2):
+            gather_up(2 * it + n, sets[n])
+            prepare(2 * it + n + 1, sets[1 - n])
         return carry
 
-    lax.fori_loop(0, (total + UNROLL - 1) // UNROLL, step, 0)
+    lax.fori_loop(0, (batches + 1) // 2, step, 0)
 
     def turned(lam, carry):
-        chunks = 2 * width // LANES
-        top = [acc[c, pl.ds(lam, half_tiles, stride=PITCH), :] for c in range(2 * chunks)]
-        low = [acc[c, pl.ds(SUB + lam, half_tiles, stride=PITCH), :] for c in range(2 * chunks)]
-        re = jnp.concatenate([top[c] - low[chunks + c] for c in range(chunks)], axis=1)
-        im = jnp.concatenate([top[chunks + c] + low[c] for c in range(chunks)], axis=1)
-        keep_ref[lam] = jnp.concatenate([re[:, :width], im[:, :width]], axis=0).astype(jnp.bfloat16)
-        give_ref[lam] = jnp.concatenate([re[:, width:], im[:, width:]], axis=0).astype(jnp.bfloat16)
+        top = [acc[c, pl.ds(lam, half_tiles, stride=PITCH), :] for c in range(2 * m_parts)]
+        low = [acc[c, pl.ds(SUB + lam, half_tiles, stride=PITCH), :] for c in range(2 * m_parts)]
+        re = [top[c] - low[m_parts + c] for c in range(m_parts)]
+        im = [top[m_parts + c] + low[c] for c in range(m_parts)]
+        if width < LANES:
+            re = [re[0][:, :width], re[0][:, width:]]
+            im = [im[0][:, :width], im[0][:, width:]]
+        whole = [jnp.concatenate(x, axis=0).astype(jnp.bfloat16) for x in zip(re, im)]
+        parts = len(whole) // 2
+        for c in range(parts):
+            keep_ref[c, lam] = whole[c]
+            give_ref[c, lam] = whole[parts + c]
         return carry
 
     lax.fori_loop(0, SUB, turned, 0, unroll=4)
@@ -362,7 +437,7 @@
     width, share, places, depths, own_ref, came_ref, head_ref, table, y_ref, out_ref, mid, out_t
 ):
     def head(lam, carry):
-        rhs = jnp.concatenate([own_ref[lam], came_ref[lam]], axis=0)
+        rhs = jnp.concatenate([own_ref[0, lam], came_ref[0, lam]], axis=0)
         got = jnp.dot(head_ref[...], rhs, preferred_element_type=jnp.float32)
         for c, rows in enumerate(in_lanes(got)):
             mid[c, pl.ds(lam * PITCH, 128), :] = rows
@@ -388,6 +463,121 @@
         width, share, (places[0], depths[0], places[1]), lambda l0: y_ref[l0], table, out_t
     )
     turn_out(out_t, out_ref)
+
+
+def finish_kernel(
+    width, places, depths, keep_ref, give_ref, head_all, table,
+    out_ref, came, mid, y_buf, away, other, out_t, core_send, core_recv, far_send, far_recv,
+):
+    uv = lax.axis_index("uv")
+    wa = lax.axis_index("wa")
+    near = {"uv": uv + 1 - 2 * lax.rem(uv, 2)}
+    far = {"wa": 1 - wa}
+    mesh_type = pl.DeviceIdType.MESH
+    barrier = pltpu.get_barrier_semaphore()
+    pl.semaphore_signal(barrier, inc=1, device_id=near, device_id_type=mesh_type)
+    pl.semaphore_signal(barrier, inc=1, device_id=far, device_id_type=mesh_type)
+    pl.semaphore_wait(barrier, 2)
+
+    parts = width // LANES
+    lam_step = SUB // SWAPS
+    swaps = []
+    for c in range(parts):
+        for k in range(SWAPS):
+            at = pl.ds(k * lam_step, lam_step)
+            n = c * SWAPS + k
+            swaps.append(
+                pltpu.make_async_remote_copy(
+                    src_ref=give_ref.at[c, at],
+                    dst_ref=came.at[c, at],
+                    send_sem=core_send.at[n],
+                    recv_sem=core_recv.at[n],
+                    device_id=near,
+                    device_id_type=mesh_type,
+                )
+            )
+            swaps[-1].start()
+    core = lax.rem(uv, 2)
+
+    share = SUB // 2
+    step = 64 // SENDS
+
+    def screened(c, l0, part, z):
+        l1 = part * share + lax.broadcasted_iota(jnp.int32, (share, LANES), 0)
+        l = l0 + 64 * l1 - G // 2
+        m = places[1] + c * LANES + lax.broadcasted_iota(jnp.int32, (share, LANES), 1)
+        x = l.astype(jnp.float32) * (1.0 / G)
+        y = m.astype(jnp.float32) * (1.0 / G)
+        ramp = jnp.bitwise_and(-(G - SUB + 1) * l, 2 * G - 1).astype(jnp.float32) * (0.5 / G)
+        sc, ss = cos_sin_turns(depths[0] * (jnp.sqrt(1.0 - y * y - x * x) - 1.0) + ramp)
+        return z[:, :LANES] * sc - z[:, LANES:] * ss
+
+    sends = []
+    for c in range(parts):
+
+        def head(lam, carry, c=c):
+            rhs = jnp.concatenate([keep_ref[c, lam], came[c, lam]], axis=0)
+            mid[c, pl.ds(lam * PITCH, 128), :] = jnp.dot(
+                head_all[core], rhs, preferred_element_type=jnp.float32
+            )
+            return carry
+
+        for k in range(SWAPS):
+            swaps[c * SWAPS + k].wait_recv()
+            lax.fori_loop(k * lam_step, (k + 1) * lam_step, head, 0, unroll=4)
+
+        def away_rows(l0, carry, c=c):
+            y = jnp.concatenate(
+                [mid[c, pl.ds(first + l0, SUB, stride=PITCH), :] for first in (0, 64)], axis=1
+            ).astype(jnp.bfloat16)
+            y_buf[c, l0] = y
+            z = jnp.dot(table[1 - wa, l0], y, preferred_element_type=jnp.float32)
+            away[c, l0] = screened(c, l0, 1 - places[0], z).astype(jnp.bfloat16)
+            return carry
+
+        for k in range(SENDS):
+            lax.fori_loop(k * step, (k + 1) * step, away_rows, 0, unroll=4)
+            at = pl.ds(k * step, step)
+            n = c * SENDS + k
+            sends.append(
+                pltpu.make_async_remote_copy(
+                    src_ref=away.at[c, at],
+                    dst_ref=other.at[c, at],
+                    send_sem=far_send.at[n],
+                    recv_sem=far_recv.at[n],
+                    device_id=far,
+                    device_id_type=mesh_type,
+                )
+            )
+            sends[-1].start()
+
+    for c in range(parts):
+
+        def own_rows(l0, carry, c=c):
+            z = jnp.dot(table[wa, l0], y_buf[c, l0], preferred_element_type=jnp.float32)
+            out_t[c, pl.ds(l0, share, stride=OUT_PITCH), :] = screened(c, l0, places[0], z)
+            return carry
+
+        lax.fori_loop(0, 64, own_rows, 0, unroll=4)
+
+    for c in range(parts):
+
+        def add_rows(l0, carry, c=c):
+            at = pl.ds(l0, share, stride=OUT_PITCH)
+            out_t[c, at, :] += other[c, l0].astype(jnp.float32)
+            return carry
+
+        for k in range(SENDS):
+            sends[c * SENDS + k].wait_recv()
+            lax.fori_loop(k * step, (k + 1) * step, add_rows, 0, unroll=4)
+
+        for n in range(share // 2):
+            rows = [out_t[c, pl.ds((2 * n + h) * OUT_PITCH, 64), :] for h in range(2)]
+            out_ref[c * LANES : (c + 1) * LANES, n * LANES : (n + 1) * LANES] = jnp.concatenate(
+                rows, axis=0
+            ).T
+    for one in swaps + sends:
+        one.wait_send()
 
 
 def on_device(visibility, coords, tile_row, col_offset, live_count):
@@ -412,49 +602,50 @@
     packed = jnp.concatenate(
         [visibility[:, 0], visibility[:, 1], coords[:, 0], coords[:, 1], numbers], axis=0
     )
-    columns = jnp.asarray(column_table())
-    d_table = jnp.concatenate(
-        [
-            lax.dynamic_slice_in_dim(columns, uv_index * width, width, 1),
-            lax.dynamic_slice_in_dim(columns, partner * width, width, 1),
-        ],
-        axis=1,
-    )
     m_first = uv_index * width - G // 2
     m_both = jnp.concatenate(
         [m_first + jnp.arange(width), partner * width + jnp.arange(width) - G // 2]
-    )[None, :]
+    )[None, :].astype(jnp.float32) * (0.5 / G)
     all_data = gather_all(packed, uv_count)
     came_numbers = all_data[:, 4 * blocks : 4 * blocks + 4, :blocks].astype(jnp.int32)
     tiles = came_numbers[:, 0]
     live = jnp.arange(blocks)[None, :] < came_numbers[:, 3]
     mine = live & (jnp.mod(tiles, 2) == core)
     homes = jnp.where(mine, tiles // 2, G // SUB // 2).reshape(-1)
-    cols = (came_numbers[:, 1] * SUB + came_numbers[:, 2])[:, :, None]
-
-    rows = packed.shape[0]
+    cols = 2 * (came_numbers[:, 1] * SUB + came_numbers[:, 2]) - (G - SUB + 1)
+    cols = cols[:, :, None].astype(jnp.float32)
+
     half_tiles = G // SUB // 2
     cap = 2 * uv_count
-    shape = (SUB, SUB, width)
+    shape = (lane_chunks(width), SUB, SUB, min(width, LANES))
     vmem = pl.BlockSpec(memory_space=pltpu.VMEM)
     smem = pl.BlockSpec(memory_space=pltpu.SMEM)
+    m_parts = 2 * width // LANES
+    k_parts = k_len // LANES
+    buffers = [
+        pltpu.VMEM((2, 2, k_parts, 72, LANES), jnp.float32),
+        pltpu.VMEM((8, k_parts, BATCH, LANES), jnp.float32),
+        pltpu.VMEM((3, k_parts, BATCH, LANES), jnp.float32),
+        pltpu.VMEM((3, m_parts, BATCH, LANES), jnp.float32),
+    ]
     own, give = pl.pallas_call(
-        functools.partial(grid_kernel, width, blocks),
+        functools.partial(grid_kernel, width, blocks, k_len),
         out_shape=[jax.ShapeDtypeStruct(shape, jnp.bfloat16)] * 2,
         in_specs=[smem, vmem, vmem, vmem, vmem],
         out_specs=[vmem, vmem],
         scratch_shapes=[
-            pltpu.VMEM((4 * width // LANES, half_tiles * PITCH, LANES), jnp.float32),
-            pltpu.VMEM((uv_count, rows, k_len), jnp.float32),
-            pltpu.VMEM((uv_count, 2, blocks, 2 * width), jnp.float32),
+            pltpu.VMEM((2 * m_parts, half_tiles * PITCH, LANES), jnp.float32),
+            pltpu.VMEM((k_parts, uv_count * 5 * blocks, LANES), jnp.float32),
             pltpu.SMEM((half_tiles * cap + uv_count * blocks,), jnp.int32),
             pltpu.SMEM((half_tiles + 1,), jnp.int32),
             pltpu.SMEM((3 * (uv_count * blocks // STACK + half_tiles),), jnp.int32),
-        ],
-        compiler_params=pltpu.CompilerParams(vmem_limit_bytes=48 * 1024 * 1024),
-    )(homes, all_data, cols, m_both, d_table)
-    came_half = lax.ppermute(give, "uv", [(n, n ^ 1) for n in range(uv_count)])
-
+            pltpu.VMEM((SUB, 2 * width), jnp.float32),
+            pltpu.VMEM((5, k_parts, BATCH, LANES), jnp.float32),
+        ]
+        + buffers
+        + buffers,
+        compiler_params=pltpu.CompilerParams(vmem_limit_bytes=32 * 1024 * 1024),
+    )(homes, all_data, cols, m_both, jnp.asarray(column_table(uv_count)))
     share = 64 // wa_count
     depth = ((wa_index.astype(jnp.float32) - (wa_count - 1) / 2.0) * plane_step)[None]
     tables = jnp.asarray(row_table(wa_count))
@@ -491,10 +682,37 @@
             compiler_params=pltpu.CompilerParams(vmem_limit_bytes=40 * 1024 * 1024),
         )(places_of(part), depth, first, tables[part])
 
-    if wa_count == 2:
-        first, away = head_of(1 - wa_index, jnp.bfloat16)
-        came = lax.ppermute(away, "wa", [(0, 1), (1, 0)])
-        return tail_of(wa_index, first, jnp.float32) + came.astype(jnp.float32)
+    if wa_count == 2 and width % LANES == 0:
+        parts = width // LANES
+        scratch = [
+            pltpu.VMEM(shape, jnp.bfloat16),
+            pltpu.VMEM((parts, SUB * PITCH, LANES), jnp.float32),
+            pltpu.VMEM((parts, 64, SUB, 2 * LANES), jnp.bfloat16),
+            pltpu.VMEM((parts, 64, share, LANES), jnp.bfloat16),
+            pltpu.VMEM((parts, 64, share, LANES), jnp.bfloat16),
+            pltpu.VMEM((parts, share * OUT_PITCH, LANES), jnp.float32),
+        ]
+        scratch += [pltpu.SemaphoreType.DMA((parts * SWAPS,))] * 2
+        scratch += [pltpu.SemaphoreType.DMA((parts * SENDS,))] * 2
+        return pl.pallas_call(
+            functools.partial(finish_kernel, width),
+            out_shape=jax.ShapeDtypeStruct((width, span), jnp.float32),
+            in_specs=[smem, smem] + [vmem] * 4,
+            out_specs=vmem,
+            scratch_shapes=scratch,
+            compiler_params=pltpu.CompilerParams(
+                collective_id=1, has_side_effects=True, vmem_limit_bytes=24 * 1024 * 1024
+            ),
+        )(
+            places_of(wa_index),
+            depth,
+            own,
+            give,
+            jnp.asarray(head_matrices()),
+            tables,
+        )
+    came_half = lax.ppermute(give, "uv", [(n, n ^ 1) for n in range(uv_count)])
+
     first, part = head_of(jnp.int32(0), jnp.bfloat16)
     images = [part] + [tail_of(jnp.int32(n), first, jnp.bfloat16) for n in range(1, wa_count)]
     parts = jnp.stack(images, axis=1)

time: 113 us -> 94.2 us (0.83)
  waiting for transfers between devices: 21.3 us -> 0 us
  Pallas kernels: 82 us -> 87.6 us
  other arithmetic: 3.26 us -> 1.58 us
  starting transfers between devices: 1.57 us -> 0 us
    ppermute x2 -> x0, waiting for transfers between devices: 21.3 us -> none  [the longest x1 17 us: on_device(): came = lax.ppermute(away, 'wa', [(0, 1), (1, 0)])]
    pallas_call x3 -> x2, Pallas kernels: 61.2 us -> 66.8 us  [the longest x1 33.5 us: on_device(): pl.pallas_call(functools.partial(grid_kernel, width, blocks, k_len), out_...]
    add x1, other arithmetic: 1.6 us -> 0.01 us  [on_device(): m_first + jnp.arange(width)]
    ppermute x2 -> x0, starting transfers between devices: 1.57 us -> none  [the longest x1 1.57 us: on_device(): came = lax.ppermute(away, 'wa', [(0, 1), (1, 0)])]
  transfers between devices with their start and end apart: 2 -> 0, of which waited for: 2 -> 0; matrix products, arithmetic and copies ran while one was open for 0% -> 0% of each run, Pallas kernels for 6% -> 0%
where the time goes in v2:
time: 94.2 us; the launch traced here: 93.9 us
  Pallas kernels  87.6 us (93%)
  local copies, waits for them, and re-layouts  3.81 us (4%)
  other arithmetic  1.58 us (2%)
    pallas_call x1, Pallas kernels, on_device(): pl.pallas_call(functools.partial(grid_kernel, width, blocks, k_len), out_...  33.5 us
    pallas_call x1, Pallas kernels, on_device(): pl.pallas_call(functools.partial(finish_kernel, width), out_shape=jax.Sha...  33.2 us
    pallas_call x1, Pallas kernels, gather_all(): pl.pallas_call(functools.partial(gather_kernel, far, near), out_shape=jax...  20.8 us

profile of v2, /device:TPU:0, one launch (start us, length us, event | category | flops | bytes accessed | tf_op | source)
XLA Modules:
  0.0 93.9 jit_solution(15386014059213499203)
XLA Ops:
  0.0 0.0 copy-start
  0.7 0.1 pad.11.clone
  0.8 0.1 pad_add_fusion.places
  0.9 0.7 convert_bitcast_fusion.1
  1.6 0.7 convert_bitcast_fusion
  2.2 0.1 maximum_maximum_fusion
  2.3 0.1 lt.30
  2.4 1.0 %fusion.14 = (bf16[48,1,256]{2,1,0:T(2,128)(2,1)S(1)}, bf16[48,1,256]{2,1,0:T(2,128)(2,1)S(1)}) fusion(bf16[48,2,256]{2,1,0:T(2,128)(2,1)} %param.8), kind=kLoop, calls=%fused_computation.43 | loop fusion | bytes 98304 | tf_op jit(solution)/shard_map/slice | solution.py:603
  3.4 1.0 %fusion.13 = (bf16[48,1,256]{2,1,0:T(2,128)(2,1)S(1)}, bf16[48,1,256]{2,1,0:T(2,128)(2,1)S(1)}) fusion(bf16[48,2,256]{2,1,0:T(2,128)(2,1)} %param.9), kind=kLoop, calls=%fused_computation.42 | loop fusion | bytes 98304 | tf_op jit(solution)/shard_map/slice | solution.py:603
  4.4 20.8 %shard_map.82.data_ref = bf16[16,208,256]{2,1,0:T(8,128)(2,1)S(1)} custom-call(bf16[208,256]{1,0:T(8,128)(2,1)S(1)} %constant_dynamic-update-slice_fusion.x_ref), custom_call_target="tpu_custom_call" | custom-call | tf_op jit(solution)/shard_map/pallas_call | solution.py:187
  25.2 0.0 copy-start.2
  25.3 0.1 slice_reduce_fusion.1
  25.3 0.1 squeeze.28
  25.4 0.1 squeeze.29
  25.5 0.2 copy.18.cols_ref
  25.7 0.0 copy-done
  25.7 0.0 copy-start.1
  25.7 33.5 %shard_map.83 = (bf16[2,64,64,128]{3,2,1,0:T(8,128)(2,1)S(1)}, bf16[2,64,64,128]{3,2,1,0:T(8,128)(2,1)S(1)}) custom-call(s32[768]{0:T(1024)S(1)} %fusion.6.homes, bf16[16,208,256]{2,1,0:T(8,128)(2,1)S(1)} %shard_map.82.data_ref, f32[16,48,1]{2,1,0:T(8,128)S(1)} %copy.18.cols_ref, f32[1,512]{1,0:T(1,128)S(1)} %fusion.10.m_ref, f32[16,64,256]{2,1,0:T(8,128)S(1)} %copy-done), custom_call_target="tpu_custom_call" | custom-call | tf_op jit(solution)/shard_map/pallas_call | solution.py:631
  59.3 0.0 copy-done.2
  59.3 0.0 copy-done.1
  59.3 33.2 %shard_map.84 = f32[256,2048]{1,0:T(8,128)S(1)} custom-call(s32[2]{0:T(128)S(1)} %pad_add_fusion.places, f32[1]{0:T(128)} %bitcast.2.depths, bf16[2,64,64,128]{3,2,1,0:T(8,128)(2,1)S(1)} %get-tuple-element.7.keep_ref, bf16[2,64,64,128]{3,2,1,0:T(8,128)(2,1)S(1)} %get-tuple-element.8.give_ref, bf16[2,128,128]{2,1,0:T(8,128)(2,1)S(1)} %copy-done.2, ...), custom_call_target="tpu_custom_call" | custom-call | tf_op jit(solution)/shard_map/pallas_call | solution.py:697
  92.6 1.3 %copy.41 = f32[256,2048]{1,0:T(8,128)} copy(f32[256,2048]{1,0:T(8,128)S(1)} %shard_map.84) | data formatting | bytes 4194304
  (11 shorter events, 0.1 us)
Async XLA Ops:
  0.0 25.7 %copy-start = (f32[16,64,256]{2,1,0:T(8,128)S(1)}, f32[16,64,256]{2,1,0:T(8,128)}, u32[]{:S(2)}) copy-start(f32[16,64,256]{2,1,0:T(8,128)} %constant.97.clone.d_all) | copy-start | bytes 3145732
  25.2 34.1 %copy-start.2 = (bf16[2,128,128]{2,1,0:T(8,128)(2,1)S(1)}, bf16[2,128,128]{2,1,0:T(8,128)(2,1)}, u32[]{:S(2)}) copy-start(bf16[2,128,128]{2,1,0:T(8,128)(2,1)} %constant.99.clone.head_all) | copy-start | bytes 196612
  25.7 33.6 %copy-start.1 = (bf16[2,64,32,64]{3,2,1,0:T(8,128)(2,1)S(1)}, bf16[2,64,32,64]{3,2,1,0:T(8,128)(2,1)}, u32[]{:S(2)}) copy-start(bf16[2,64,32,64]{3,2,1,0:T(8,128)(2,1)} %constant.98.clone.table) | copy-start | bytes 1572868

commit v3 on v2

--- a/solution.py
+++ b/solution.py
@@ -13,6 +13,7 @@
 G = 4096
 SUB = 64
 BATCH = 8
+PLACES = 8
 STACK = 4
 LANES = 128
 PITCH = 129
@@ -114,76 +115,151 @@
     return np.stack(out).astype(BF)
 
 
-def gather_kernel(far, near, x_ref, out_ref, z_send, z_recv, y_send, y_recv, c_send, c_recv):
-    me = lax.axis_index("uv")
-    c = lax.rem(me, 2)
-    b = lax.rem(me // 2, near)
-    a = me // (2 * near)
+def gather_kernel(
+    far, near, x_ref, out_ref,
+    own_sem, ring_send, ring_recv, side_send, side_recv, core_send, core_recv,
+):
+    uv = lax.axis_index("uv")
+    c = lax.rem(uv, 2)
+    b = lax.rem(uv // 2, near)
+    a = uv // (2 * near)
+    mesh_type = pl.DeviceIdType.MESH
+    sources = (x_ref,)
+    outs = (out_ref,)
 
     def at(da, db, dc):
-        return (
-            lax.rem(a + da + far, far) * near + lax.rem(b + db + near, near)
-        ) * 2 + lax.rem(c + dc, 2)
-
-    peers = [at(d, 0, 0) for d in range(1, far)]
-    peers += [at(0, e, 0) for e in range(1, near)] + [at(0, 0, 1)]
+        return ((a + da) * near + lax.rem(b + db + near, near)) * 2 + lax.rem(c + dc, 2)
+
+    def inside(da):
+        return jnp.logical_and(a + da >= 0, a + da < far)
+
     barrier = pltpu.get_barrier_semaphore()
-    for peer in peers:
-        pl.semaphore_signal(
-            barrier, inc=1, device_id={"uv": peer}, device_id_type=pl.DeviceIdType.MESH
-        )
-    pl.semaphore_wait(barrier, len(peers))
-
-    def copy(source, slot, target, send, recv):
+
+    def greet(device):
+        pl.semaphore_signal(barrier, inc=1, device_id={"uv": device}, device_id_type=mesh_type)
+
+    for side in (-1, 1):
+        pl.when(inside(side))(lambda side=side: greet(at(side, 0, 0)))
+    for e in range(1, near):
+        greet(at(0, e, 0))
+    greet(at(0, 0, 1))
+    mine = [
+        pltpu.make_async_copy(sources[k], outs[k].at[uv], own_sem.at[k]) for k in range(1)
+    ]
+    for one in mine:
+        one.start()
+    beside = jnp.where(a > 0, 1, 0) + jnp.where(a < far - 1, 1, 0)
+    pl.semaphore_wait(barrier, beside + near)
+
+    def copy(k, own, slot, target, send, recv):
         return pltpu.make_async_remote_copy(
-            src_ref=source,
-            dst_ref=out_ref.at[slot],
+            src_ref=sources[k] if own else outs[k].at[slot],
+            dst_ref=outs[k].at[slot],
             send_sem=send,
             recv_sem=recv,
             device_id={"uv": target},
-            device_id_type=pl.DeviceIdType.MESH,
+            device_id_type=mesh_type,
         )
 
-    sent = []
-
-    def send(source, slot, target, send_sem, recv_sem):
-        one = copy(source, slot, target, send_sem, recv_sem)
-        one.start()
-        sent.append(one)
-
-    for d in range(1, far):
-        send(x_ref, me, at(d, 0, 0), z_send.at[d], z_recv.at[d])
-    for d in range(far):
-        slot = at(-d, 0, 0)
-        source = x_ref if d == 0 else out_ref.at[slot]
-        if d > 0:
-            copy(x_ref, slot, me, z_send.at[d], z_recv.at[d]).wait_recv()
+    first = (0,)
+    second = ()
+    sends = []
+
+    def start(valid, one):
+        pl.when(valid)(lambda: one.start())
+        sends.append((valid, one))
+
+    def along(k, da, e, own):
+        slot = at(da, -e, 0)
+        if da <= 0:
+            n = (k * near + e) * 2 * far - da
+            start(
+                jnp.logical_and(inside(da), inside(1)),
+                copy(k, own, slot, at(1, 0, 0), ring_send.at[n], ring_recv.at[n + 1]),
+            )
+        if da >= 0:
+            n = ((k * near + e) * 2 + 1) * far + da
+            start(
+                jnp.logical_and(inside(da), inside(-1)),
+                copy(k, own, slot, at(-1, 0, 0), ring_send.at[n], ring_recv.at[n + 1]),
+            )
+
+    def arrived_along(k, da, e):
+        slot = at(da, -e, 0)
+        n = (k * near + e) * 2 * far - da if da < 0 else ((k * near + e) * 2 + 1) * far + da
+        one = copy(k, False, slot, uv ^ 1, ring_send.at[n], ring_recv.at[n])
+        pl.when(inside(da))(lambda: one.wait_recv())
+
+    def aside(k, da, own):
         for e in range(1, near):
-            k = d * near + e
-            send(source, slot, at(0, e, 0), y_send.at[k], y_recv.at[k])
-        k = d * near
-        send(source, slot, at(0, 0, 1), c_send.at[k], c_recv.at[k])
-        if d == 0:
-            out_ref[me] = x_ref[...]
-    for d in range(far):
-        for e in range(1, near):
-            k = d * near + e
-            slot = at(-d, -e, 0)
-            copy(x_ref, slot, me, y_send.at[k], y_recv.at[k]).wait_recv()
-            send(out_ref.at[slot], slot, at(0, 0, 1), c_send.at[k], c_recv.at[k])
-    for d in range(far):
+            n = (k * (2 * far) + far + da) * near + e
+            start(
+                inside(da),
+                copy(k, own, at(da, 0, 0), at(0, e, 0), side_send.at[n], side_recv.at[n]),
+            )
+
+    def arrived_aside(k, da, e):
+        n = (k * (2 * far) + far + da) * near + e
+        one = copy(k, False, at(da, -e, 0), uv ^ 1, side_send.at[n], side_recv.at[n])
+        pl.when(inside(da))(lambda: one.wait_recv())
+
+    def across(k, da, e, own):
+        n = (k * (2 * far) + far + da) * near + e
+        start(
+            inside(da),
+            copy(k, own, at(da, -e, 0), at(0, 0, 1), core_send.at[n], core_recv.at[n]),
+        )
+
+    for k in second:
+        aside(k, 0, True)
+    for k in first:
+        along(k, 0, 0, True)
+    for k in second:
+        along(k, 0, 0, True)
+    for k in first:
+        aside(k, 0, True)
+    for k in range(1):
+        across(k, 0, 0, True)
+    for e in range(1, near):
+        for k in second:
+            arrived_aside(k, 0, e)
+            along(k, 0, e, False)
+            across(k, 0, e, False)
+    for s in range(1, far):
+        for k in first:
+            for da in (-s, s):
+                arrived_along(k, da, 0)
+                along(k, da, 0, False)
+                aside(k, da, False)
+                across(k, da, 0, False)
         for e in range(near):
-            k = d * near + e
-            copy(x_ref, at(-d, -e, 1), me, c_send.at[k], c_recv.at[k]).wait_recv()
-    for one in sent:
-        one.wait_send()
+            for k in second:
+                for da in (-s, s):
+                    arrived_along(k, da, e)
+                    along(k, da, e, False)
+                    across(k, da, e, False)
+    for k in first:
+        for da in sorted(range(1 - far, far), key=abs):
+            for e in range(1, near):
+                arrived_aside(k, da, e)
+                across(k, da, e, False)
+    for da in sorted(range(1 - far, far), key=abs):
+        for e in range(near):
+            for k in range(1):
+                n = (k * (2 * far) + far + da) * near + e
+                one = copy(k, False, at(da, -e, 1), uv ^ 1, core_send.at[n], core_recv.at[n])
+                pl.when(inside(da))(lambda one=one: one.wait_recv())
+    for one in mine:
+        one.wait()
+    for valid, one in sends:
+        pl.when(valid)(lambda one=one: one.wait_send())
 
 
 def gather_all(packed, uv_count):
     chips = uv_count // 2
     near = 1 << ((chips.bit_length() - 1) // 2)
     far = chips // near
-    sems = [far] * 2 + [far * near] * 4
+    sems = [1] + [near * 2 * far + 1] * 2 + [2 * far * near] * 4
     return pl.pallas_call(
         functools.partial(gather_kernel, far, near),
         out_shape=jax.ShapeDtypeStruct((uv_count,) + packed.shape, packed.dtype),
@@ -191,28 +267,33 @@
         out_specs=pl.BlockSpec(memory_space=pltpu.VMEM),
         scratch_shapes=[pltpu.SemaphoreType.DMA((n,)) for n in sems],
         compiler_params=pltpu.CompilerParams(
-            collective_id=0, has_side_effects=True, vmem_limit_bytes=24 * 1024 * 1024
+            collective_id=0, has_side_effects=True, vmem_limit_bytes=16 * 1024 * 1024
         ),
     )(packed)
 
 
 def grid_kernel(
-    width, blocks, k_len, homes, data_ref, cols_ref, m_ref, d_all, keep_ref, give_ref,
-    acc, rows_f, slots, filled, group, d_ref, *buffers,
+    width, blocks, homes, cols, counts, data_ref, m_ref, d_all, keep_ref, give_ref,
+    acc, slots, filled, fours, twos, d_ref, *buffers,
 ):
-    devices = data_ref.shape[0]
+    each = 2 * blocks + 2
+    devices = data_ref.shape[0] // each
+    k_len = data_ref.shape[2]
     cap = 2 * devices
     half_tiles = G // SUB // 2
     both = 2 * width
     k_parts = k_len // LANES
     m_parts = both // LANES
-    each = 5 * blocks
     uv = lax.axis_index("uv")
     stage = buffers[0]
     sets = (buffers[1:5], buffers[5:9])
     d_ref[:, :width] = d_all[uv]
     d_ref[:, width:] = d_all[uv + 1 - 2 * lax.rem(uv, 2)]
 
+    for n in range(3):
+        fours[n] = 0
+        twos[n] = 0
+
     def empty(h, carry):
         filled[h] = 0
         return carry
@@ -224,53 +305,62 @@
         at = jnp.minimum(j * clear, half_tiles * PITCH - clear)
         for c in range(2 * m_parts):
             acc[c, pl.ds(at, clear), :] = jnp.zeros((clear, LANES), jnp.float32)
-        base = pl.multiple_of(j * each, 8)
-        for c in range(k_parts):
-            rows_f[c, pl.ds(base, 4 * blocks), :] = data_ref[
-                j, : 4 * blocks, c * LANES : (c + 1) * LANES
-            ].astype(jnp.float32)
-        rows_f[0, pl.ds(base + 4 * blocks, blocks), :] = jnp.broadcast_to(
-            cols_ref[j], (blocks, LANES)
-        )
-        for i in range(blocks):
-            h = homes[j * blocks + i]
-            n = filled[h]
-            slots[h * cap + n] = j * each + i
-            filled[h] = n + 1
-        return carry
+        def place(n, inner):
+            for k in range(PLACES):
+                i = n * PLACES + k
+                h = homes[j * blocks + i]
+                n_h = filled[h]
+                slots[h * cap + n_h] = j * each + i
+                filled[h] = n_h + 1
+            return inner
+
+        return lax.fori_loop(0, (counts[j] + PLACES - 1) // PLACES, place, carry)
 
     lax.fori_loop(0, devices, spread, 0)
 
     def list_groups(h, found):
+        count = filled[h]
+        whole = (count + 1) // STACK
+
         def one(g, n):
-            group[3 * n] = h
-            group[3 * n + 1] = h * cap + STACK * g
-            group[3 * n + 2] = filled[h] - STACK * g
+            fours[3 * n] = h
+            fours[3 * n + 1] = h * cap + STACK * g
+            fours[3 * n + 2] = count - STACK * g
             return n + 1
 
-        return lax.fori_loop(0, (filled[h] + STACK - 1) // STACK, one, found)
-
-    total = lax.fori_loop(0, half_tiles, list_groups, 0)
+        n, m = found
+        n = lax.fori_loop(0, whole, one, n)
+        rest = count - STACK * whole
+        twos[3 * m] = h
+        twos[3 * m + 1] = h * cap + STACK * whole
+        twos[3 * m + 2] = rest
+        return n, m + jnp.where(rest > 0, 1, 0)
+
+    n_fours, n_twos = lax.fori_loop(0, half_tiles, list_groups, (0, 0))
     scale = 1.0 / math.sqrt(k_len)
 
-    def prepare(batch, refs):
+    def prepare(batch, refs, stack, group, total):
         fine, coarse, signal, phase = refs
-        for p in range(BATCH // STACK):
-            n = batch * (BATCH // STACK) + p
+        for p in range(BATCH // stack):
+            n = batch * (BATCH // stack) + p
             real = n < total
             n = jnp.where(real, n, 0)
             first = group[3 * n + 1]
             left_over = jnp.where(real, group[3 * n + 2], 0)
-            for q in range(STACK):
+            for q in range(stack):
                 live = q < left_over
                 row = jnp.where(live, slots[first + q], 0)
+                centre = (2 * cols[row] - (G - SUB + 1)).astype(jnp.float32)
                 keep = jnp.where(live, scale, 0.0)
-                k = p * STACK + q
+                k = p * stack + q
+                signals = data_ref[row].astype(jnp.float32) * keep
+                places = data_ref[row + blocks].astype(jnp.float32)
                 for c in range(k_parts):
-                    for r in range(4):
-                        value = rows_f[c, pl.ds(row + r * blocks, 1), :]
-                        stage[r, c, k : k + 1, :] = value * keep if r < 2 else value
-                stage[4, 0, k : k + 1, :] = rows_f[0, pl.ds(row + 4 * blocks, 1), :]
+                    cut = slice(c * LANES, (c + 1) * LANES)
+                    for r in range(2):
+                        stage[r, c, k : k + 1, :] = signals[r : r + 1, cut]
+                        stage[2 + r, c, k : k + 1, :] = places[r : r + 1, cut]
+                stage[4, 0, k : k + 1, :] = jnp.full((1, LANES), centre, jnp.float32)
         for c in range(k_parts):
             halves = []
             for axis in range(2):
@@ -331,25 +421,30 @@
             preferred_element_type=jnp.float32,
         ).astype(jnp.bfloat16)
 
-    def gather_up(batch, refs):
+    def gather_up(batch, refs, stack, group, total):
         phase = refs[3]
-        for p in range(BATCH // STACK):
-            n = batch * (BATCH // STACK) + p
+        pieces = [
+            jnp.concatenate([piece_of(k, refs) for k in range(p * stack, (p + 1) * stack)], axis=1)
+            for p in range(BATCH // stack)
+        ]
+        for p in range(BATCH // stack):
+            n = batch * (BATCH // stack) + p
             h = group[3 * jnp.where(n < total, n, 0)]
             rows = pl.ds(h * PITCH, 2 * SUB)
-            ks = range(p * STACK, (p + 1) * STACK)
-            piece = jnp.concatenate([piece_of(k, refs) for k in ks], axis=1)
+            ks = range(p * stack, (p + 1) * stack)
+            piece = pieces[p]
             wide = min(2, m_parts)
             for c0 in range(0, m_parts, wide):
+                tops = [d_ref[:32, c * LANES : (c + 1) * LANES] for c in range(c0, c0 + wide)]
+                lows = [d_ref[32:, c * LANES : (c + 1) * LANES] for c in range(c0, c0 + wide)]
                 for turn in range(2):
                     weight = []
                     for k in ks:
                         top, low = [], []
                         for c in range(c0, c0 + wide):
-                            cut = slice(c * LANES, (c + 1) * LANES)
                             pr, pi, npi = (phase[e, c, k : k + 1, :] for e in range(3))
-                            top.append(d_ref[:32, cut] * (pi if turn else pr))
-                            low.append(d_ref[32:, cut] * (pr if turn else npi))
+                            top.append(tops[c - c0] * (pi if turn else pr))
+                            low.append(lows[c - c0] * (pr if turn else npi))
                         weight += [jnp.concatenate(top, axis=1), jnp.concatenate(low, axis=1)]
                     got = jnp.dot(
                         piece,
@@ -360,16 +455,24 @@
                         at = turn * m_parts + c0 + c
                         acc[at, rows, :] += got[:, c * LANES : (c + 1) * LANES]
 
-    batches = (total + BATCH // STACK - 1) // (BATCH // STACK)
-    prepare(0, sets[0])
-
-    def step(it, carry):
-        for n in range(2):
-            gather_up(2 * it + n, sets[n])
-            prepare(2 * it + n + 1, sets[1 - n])
-        return carry
-
-    lax.fori_loop(0, (batches + 1) // 2, step, 0)
+    for stack, group, total in ((STACK, fours, n_fours), (2, twos, n_twos)):
+        batches = (total + BATCH // stack - 1) // (BATCH // stack)
+        rest = (stack, group, total)
+        prepare(0, sets[0], *rest)
+
+        def step(it, carry, rest=rest):
+            for n in range(2):
+                gather_up(2 * it + n, sets[n], *rest)
+                prepare(2 * it + n + 1, sets[1 - n], *rest)
+            return carry
+
+        lax.fori_loop(0, batches // 2, step, 0)
+
+        def last(it, carry, rest=rest, batches=batches):
+            gather_up(batches - 1, sets[0], *rest)
+            return carry
+
+        lax.fori_loop(0, lax.rem(batches, 2), last, 0)
 
     def turned(lam, carry):
         top = [acc[c, pl.ds(lam, half_tiles, stride=PITCH), :] for c in range(2 * m_parts)]
@@ -590,6 +693,10 @@
     width = G // uv_count
     core = jnp.mod(uv_index, 2)
     partner = uv_index + 1 - 2 * core
+    m_first = uv_index * width - G // 2
+    m_both = jnp.concatenate(
+        [m_first + jnp.arange(width), partner * width + jnp.arange(width) - G // 2]
+    )[None, :].astype(jnp.float32) * (0.5 / G)
     numbers = jnp.stack(
         [
             tile_row[:, 0],
@@ -598,23 +705,17 @@
             jnp.broadcast_to(live_count[0], (blocks,)),
         ]
     )
-    numbers = jnp.pad(numbers, ((0, 12), (0, k_len - blocks))).astype(jnp.bfloat16)
-    packed = jnp.concatenate(
-        [visibility[:, 0], visibility[:, 1], coords[:, 0], coords[:, 1], numbers], axis=0
-    )
-    m_first = uv_index * width - G // 2
-    m_both = jnp.concatenate(
-        [m_first + jnp.arange(width), partner * width + jnp.arange(width) - G // 2]
-    )[None, :].astype(jnp.float32) * (0.5 / G)
+    numbers = jnp.pad(numbers, ((0, 0), (0, k_len - blocks))).astype(jnp.bfloat16)
+    packed = jnp.concatenate([visibility, coords, numbers.reshape(2, 2, k_len)], axis=0)
     all_data = gather_all(packed, uv_count)
-    came_numbers = all_data[:, 4 * blocks : 4 * blocks + 4, :blocks].astype(jnp.int32)
-    tiles = came_numbers[:, 0]
-    live = jnp.arange(blocks)[None, :] < came_numbers[:, 3]
+    numbers = all_data[:, 2 * blocks :, :, :blocks].reshape(uv_count, 4, blocks)
+    numbers = numbers.astype(jnp.int32)
+    tiles = numbers[:, 0]
+    cols = numbers[:, 1] * SUB + numbers[:, 2]
+    cols = jnp.pad(cols, ((0, 0), (0, blocks + 2))).reshape(-1)
+    live = jnp.arange(blocks)[None, :] < numbers[:, 3]
     mine = live & (jnp.mod(tiles, 2) == core)
     homes = jnp.where(mine, tiles // 2, G // SUB // 2).reshape(-1)
-    cols = 2 * (came_numbers[:, 1] * SUB + came_numbers[:, 2]) - (G - SUB + 1)
-    cols = cols[:, :, None].astype(jnp.float32)
-
     half_tiles = G // SUB // 2
     cap = 2 * uv_count
     shape = (lane_chunks(width), SUB, SUB, min(width, LANES))
@@ -629,23 +730,30 @@
         pltpu.VMEM((3, m_parts, BATCH, LANES), jnp.float32),
     ]
     own, give = pl.pallas_call(
-        functools.partial(grid_kernel, width, blocks, k_len),
+        functools.partial(grid_kernel, width, blocks),
         out_shape=[jax.ShapeDtypeStruct(shape, jnp.bfloat16)] * 2,
-        in_specs=[smem, vmem, vmem, vmem, vmem],
+        in_specs=[smem, smem, smem, vmem, vmem, vmem],
         out_specs=[vmem, vmem],
         scratch_shapes=[
             pltpu.VMEM((2 * m_parts, half_tiles * PITCH, LANES), jnp.float32),
-            pltpu.VMEM((k_parts, uv_count * 5 * blocks, LANES), jnp.float32),
             pltpu.SMEM((half_tiles * cap + uv_count * blocks,), jnp.int32),
             pltpu.SMEM((half_tiles + 1,), jnp.int32),
             pltpu.SMEM((3 * (uv_count * blocks // STACK + half_tiles),), jnp.int32),
+            pltpu.SMEM((3 * (half_tiles + 1),), jnp.int32),
             pltpu.VMEM((SUB, 2 * width), jnp.float32),
             pltpu.VMEM((5, k_parts, BATCH, LANES), jnp.float32),
         ]
         + buffers
         + buffers,
         compiler_params=pltpu.CompilerParams(vmem_limit_bytes=32 * 1024 * 1024),
-    )(homes, all_data, cols, m_both, jnp.asarray(column_table(uv_count)))
+    )(
+        homes,
+        cols,
+        numbers[:, 3, 0],
+        all_data.reshape((-1,) + all_data.shape[2:]),
+        m_both,
+        jnp.asarray(column_table(uv_count)),
+    )
     share = 64 // wa_count
     depth = ((wa_index.astype(jnp.float32) - (wa_count - 1) / 2.0) * plane_step)[None]
     tables = jnp.asarray(row_table(wa_count))

time: 94.2 us -> 85.7 us (0.910)
  Pallas kernels: 87.6 us -> 80.2 us
  local copies, waits for them, and re-layouts: 3.81 us -> 1.86 us
  other arithmetic: 1.58 us -> 2.55 us
    pallas_call x1, Pallas kernels: 33.5 us -> 27.2 us  [on_device(): pl.pallas_call(functools.partial(grid_kernel, width, blocks), out_shape=[...]
    slice x2, local copies, waits for them, and re-layouts: 1.92 us -> 0.03 us  [the longest x1 0.01 us: on_device(): numbers = all_data[:, 2 * blocks:, :, :blocks].reshape(uv_count, 4, blocks)]
    pallas_call x1, Pallas kernels: 33.2 us -> 32.1 us  [on_device(): pl.pallas_call(functools.partial(finish_kernel, width), out_shape=jax.Sha...]
    concatenate x0 -> x1, other arithmetic: none -> 0.97 us  [on_device(): jnp.concatenate([visibility, coords, numbers.reshape(2, 2, k_len)], axis=0)]
where the time goes in v3:
time: 85.7 us; the launch traced here: 85.5 us
  Pallas kernels  80.2 us (94%)
  other arithmetic  2.55 us (3%)
  local copies, waits for them, and re-layouts  1.86 us (2%)
  between operations  0.88 us (1%)
    pallas_call x1, Pallas kernels, on_device(): pl.pallas_call(functools.partial(finish_kernel, width), out_shape=jax.Sha...  32.1 us
    pallas_call x1, Pallas kernels, on_device(): pl.pallas_call(functools.partial(grid_kernel, width, blocks), out_shape=[...  27.2 us
    pallas_call x1, Pallas kernels, gather_all(): pl.pallas_call(functools.partial(gather_kernel, far, near), out_shape=jax...  21 us

profile of v3, /device:TPU:0, one launch (start us, length us, event | category | flops | bytes accessed | tf_op | source)
XLA Modules:
  0.0 85.5 jit_solution(14796161486759650559)
XLA Ops:
  0.0 0.0 copy-start
  0.7 0.1 pad.19.clone
  0.8 0.1 pad_add_fusion.places
  0.9 0.7 convert_bitcast_fusion.1
  1.6 0.7 convert_bitcast_fusion
  2.2 0.1 maximum_maximum_fusion
  2.4 0.1 lt.30
  2.4 1.0 %pad_maximum_fusion.x_ref = bf16[98,2,256]{2,1,0:T(2,128)(2,1)S(1)} fusion(bf16[2,2,256]{2,1,0:T(2,128)(2,1)S(1)} %reshape.51, bf16[48,2,256]{2,1,0:T(2,128)(2,1)} %param.9, bf16[48,2,256]{2,1,0:T(2,128)(2,1)} %param.8), kind=kLoop, calls=%fused_computation | loop fusion | flops 100352 | bytes 200704 | tf_op jit(solution)/shard_map/concatenate | solution.py:709
  3.4 0.0 copy-start.2
  3.4 21.0 %shard_map.82 = bf16[16,98,2,256]{3,2,1,0:T(2,128)(2,1)S(1)} custom-call(bf16[98,2,256]{2,1,0:T(2,128)(2,1)S(1)} %pad_maximum_fusion.x_ref), custom_call_target="tpu_custom_call" | custom-call | tf_op jit(solution)/shard_map/pallas_call | solution.py:263
  24.4 0.1 slice_reduce_fusion.1
  24.5 0.1 copy.10
  24.6 0.1 squeeze.15
  24.7 0.1 squeeze.16
  24.8 0.1 reshape.52.cols
  24.9 0.0 copy-done
  24.9 0.0 copy-start.1
  24.9 27.2 %shard_map.83 = (bf16[2,64,64,128]{3,2,1,0:T(8,128)(2,1)S(1)}, bf16[2,64,64,128]{3,2,1,0:T(8,128)(2,1)S(1)}) custom-call(s32[768]{0:T(1024)S(1)} %fusion.1.homes, s32[1568]{0:T(1024)S(1)} %reshape.52.cols, s32[16]{0:T(128)S(1)} %bitcast.20, bf16[1568,2,256]{2,1,0:T(2,128)(2,1)S(1)} %bitcast.19, f32[1,512]{1,0:T(1,128)S(1)} %fusion.5.m_ref, ...), custom_call_target="tpu_custom_call" | custom-call | tf_op jit(solution)/shard_map/pallas_call | solution.py:732
  52.1 0.0 copy-done.2
  52.1 0.0 copy-done.1
  52.1 32.1 %shard_map.84 = f32[256,2048]{1,0:T(8,128)S(1)} custom-call(s32[2]{0:T(128)S(1)} %pad_add_fusion.places, f32[1]{0:T(128)} %bitcast.2.depths, bf16[2,64,64,128]{3,2,1,0:T(8,128)(2,1)S(1)} %get-tuple-element.7.keep_ref, bf16[2,64,64,128]{3,2,1,0:T(8,128)(2,1)S(1)} %get-tuple-element.8.give_ref, bf16[2,128,128]{2,1,0:T(8,128)(2,1)S(1)} %copy-done.2, ...), custom_call_target="tpu_custom_call" | custom-call | tf_op jit(solution)/shard_map/pallas_call | solution.py:805
  84.2 1.3 %copy.13 = f32[256,2048]{1,0:T(8,128)} copy(f32[256,2048]{1,0:T(8,128)S(1)} %shard_map.84) | data formatting | bytes 4194304
  (11 shorter events, 0.1 us)
Async XLA Ops:
  0.0 24.9 %copy-start = (f32[16,64,256]{2,1,0:T(8,128)S(1)}, f32[16,64,256]{2,1,0:T(8,128)}, u32[]{:S(2)}) copy-start(f32[16,64,256]{2,1,0:T(8,128)} %constant.93.clone.d_all) | copy-start | bytes 3145732
  3.4 48.7 %copy-start.2 = (bf16[2,128,128]{2,1,0:T(8,128)(2,1)S(1)}, bf16[2,128,128]{2,1,0:T(8,128)(2,1)}, u32[]{:S(2)}) copy-start(bf16[2,128,128]{2,1,0:T(8,128)(2,1)} %constant.95.clone.head_all) | copy-start | bytes 196612
  24.9 27.2 %copy-start.1 = (bf16[2,64,32,64]{3,2,1,0:T(8,128)(2,1)S(1)}, bf16[2,64,32,64]{3,2,1,0:T(8,128)(2,1)}, u32[]{:S(2)}) copy-start(bf16[2,64,32,64]{3,2,1,0:T(8,128)(2,1)} %constant.94.clone.table) | copy-start | bytes 1572868

commit v4 on v3

--- a/solution.py
+++ b/solution.py
@@ -14,6 +14,7 @@
 SUB = 64
 BATCH = 8
 PLACES = 8
+WIPE = 72
 STACK = 4
 LANES = 128
 PITCH = 129
@@ -299,24 +300,32 @@
         return carry
 
     lax.fori_loop(0, half_tiles + 1, empty, 0)
-    clear = max(1, half_tiles // devices) * PITCH
+    wipes = acc.shape[1] // WIPE
+
+    def wipe(n):
+        at = pl.multiple_of(jnp.minimum(n, wipes - 1) * WIPE, WIPE)
+        for c in range(2 * m_parts):
+            acc[c, pl.ds(at, WIPE), :] = jnp.zeros((WIPE, LANES), jnp.float32)
+
 
     def spread(j, carry):
-        at = jnp.minimum(j * clear, half_tiles * PITCH - clear)
-        for c in range(2 * m_parts):
-            acc[c, pl.ds(at, clear), :] = jnp.zeros((clear, LANES), jnp.float32)
         def place(n, inner):
+            wipe(inner)
             for k in range(PLACES):
                 i = n * PLACES + k
                 h = homes[j * blocks + i]
                 n_h = filled[h]
                 slots[h * cap + n_h] = j * each + i
                 filled[h] = n_h + 1
-            return inner
+            return inner + 1
 
         return lax.fori_loop(0, (counts[j] + PLACES - 1) // PLACES, place, carry)
 
-    lax.fori_loop(0, devices, spread, 0)
+    def wipe_rest(n, carry):
+        wipe(n)
+        return carry
+
+    lax.fori_loop(lax.fori_loop(0, devices, spread, 0), wipes, wipe_rest, 0)
 
     def list_groups(h, found):
         count = filled[h]
@@ -627,7 +636,7 @@
 
         for k in range(SWAPS):
             swaps[c * SWAPS + k].wait_recv()
-            lax.fori_loop(k * lam_step, (k + 1) * lam_step, head, 0, unroll=4)
+            lax.fori_loop(k * lam_step, (k + 1) * lam_step, head, 0, unroll=16)
 
         def away_rows(l0, carry, c=c):
             y = jnp.concatenate(
@@ -639,7 +648,7 @@
             return carry
 
         for k in range(SENDS):
-            lax.fori_loop(k * step, (k + 1) * step, away_rows, 0, unroll=4)
+            lax.fori_loop(k * step, (k + 1) * step, away_rows, 0, unroll=16)
             at = pl.ds(k * step, step)
             n = c * SENDS + k
             sends.append(
@@ -661,7 +670,7 @@
             out_t[c, pl.ds(l0, share, stride=OUT_PITCH), :] = screened(c, l0, places[0], z)
             return carry
 
-        lax.fori_loop(0, 64, own_rows, 0, unroll=4)
+        lax.fori_loop(0, 64, own_rows, 0, unroll=16)
 
     for c in range(parts):
 
@@ -672,7 +681,7 @@
 
         for k in range(SENDS):
             sends[c * SENDS + k].wait_recv()
-            lax.fori_loop(k * step, (k + 1) * step, add_rows, 0, unroll=4)
+            lax.fori_loop(k * step, (k + 1) * step, add_rows, 0, unroll=16)
 
         for n in range(share // 2):
             rows = [out_t[c, pl.ds((2 * n + h) * OUT_PITCH, 64), :] for h in range(2)]
@@ -735,7 +744,7 @@
         in_specs=[smem, smem, smem, vmem, vmem, vmem],
         out_specs=[vmem, vmem],
         scratch_shapes=[
-            pltpu.VMEM((2 * m_parts, half_tiles * PITCH, LANES), jnp.float32),
+            pltpu.VMEM((2 * m_parts, -(-half_tiles * PITCH // WIPE) * WIPE, LANES), jnp.float32),
             pltpu.SMEM((half_tiles * cap + uv_count * blocks,), jnp.int32),
             pltpu.SMEM((half_tiles + 1,), jnp.int32),
             pltpu.SMEM((3 * (uv_count * blocks // STACK + half_tiles),), jnp.int32),

time: 85.7 us -> 82.8 us (0.966)
  Pallas kernels: 80.2 us -> 77.6 us
    pallas_call x1, Pallas kernels: 27.2 us -> 23.5 us  [on_device(): pl.pallas_call(functools.partial(grid_kernel, width, blocks), out_shape=[...]
    pallas_call x1, Pallas kernels: 32.1 us -> 33.2 us  [on_device(): pl.pallas_call(functools.partial(finish_kernel, width), out_shape=jax.Sha...]
where the time goes in v4:
time: 82.8 us
  Pallas kernels  77.6 us (94%)
  other arithmetic  2.55 us (3%)
  local copies, waits for them, and re-layouts  1.86 us (2%)
  between operations  0.88 us (1%)
    pallas_call x1, Pallas kernels, on_device(): pl.pallas_call(functools.partial(finish_kernel, width), out_shape=jax.Sha...  33.2 us
    pallas_call x1, Pallas kernels, on_device(): pl.pallas_call(functools.partial(grid_kernel, width, blocks), out_shape=[...  23.5 us
    pallas_call x1, Pallas kernels, gather_all(): pl.pallas_call(functools.partial(gather_kernel, far, near), out_shape=jax...  21 us

profile of v4, /device:TPU:0, one launch (start us, length us, event | category | flops | bytes accessed | tf_op | source)
XLA Modules:
  0.0 82.8 jit_solution(1865947408872332536)
XLA Ops:
  0.0 0.0 copy-start
  0.7 0.1 pad.19.clone
  0.8 0.1 pad_add_fusion.places
  0.9 0.7 convert_bitcast_fusion.1
  1.6 0.7 convert_bitcast_fusion
  2.2 0.1 maximum_maximum_fusion
  2.4 0.1 lt.30
  2.4 1.0 %pad_maximum_fusion.x_ref = bf16[98,2,256]{2,1,0:T(2,128)(2,1)S(1)} fusion(bf16[2,2,256]{2,1,0:T(2,128)(2,1)S(1)} %reshape.51, bf16[48,2,256]{2,1,0:T(2,128)(2,1)} %param.9, bf16[48,2,256]{2,1,0:T(2,128)(2,1)} %param.8), kind=kLoop, calls=%fused_computation | loop fusion | flops 100352 | bytes 200704 | tf_op jit(solution)/shard_map/concatenate | solution.py:718
  3.4 0.0 copy-start.2
  3.4 21.0 %shard_map.82 = bf16[16,98,2,256]{3,2,1,0:T(2,128)(2,1)S(1)} custom-call(bf16[98,2,256]{2,1,0:T(2,128)(2,1)S(1)} %pad_maximum_fusion.x_ref), custom_call_target="tpu_custom_call" | custom-call | tf_op jit(solution)/shard_map/pallas_call | solution.py:264
  24.4 0.1 slice_reduce_fusion.1
  24.5 0.1 copy.10
  24.6 0.1 squeeze.15
  24.7 0.1 squeeze.16
  24.8 0.1 reshape.52.cols
  24.9 0.0 copy-done
  24.9 0.0 copy-start.1
  24.9 23.5 %shard_map.83 = (bf16[2,64,64,128]{3,2,1,0:T(8,128)(2,1)S(1)}, bf16[2,64,64,128]{3,2,1,0:T(8,128)(2,1)S(1)}) custom-call(s32[768]{0:T(1024)S(1)} %fusion.1.homes, s32[1568]{0:T(1024)S(1)} %reshape.52.cols, s32[16]{0:T(128)S(1)} %bitcast.20, bf16[1568,2,256]{2,1,0:T(2,128)(2,1)S(1)} %bitcast.19, f32[1,512]{1,0:T(1,128)S(1)} %fusion.5.m_ref, ...), custom_call_target="tpu_custom_call" | custom-call | tf_op jit(solution)/shard_map/pallas_call | solution.py:741
  48.3 0.0 copy-done.2
  48.3 0.0 copy-done.1
  48.4 33.2 %shard_map.84 = f32[256,2048]{1,0:T(8,128)S(1)} custom-call(s32[2]{0:T(128)S(1)} %pad_add_fusion.places, f32[1]{0:T(128)} %bitcast.2.depths, bf16[2,64,64,128]{3,2,1,0:T(8,128)(2,1)S(1)} %get-tuple-element.7.keep_ref, bf16[2,64,64,128]{3,2,1,0:T(8,128)(2,1)S(1)} %get-tuple-element.8.give_ref, bf16[2,128,128]{2,1,0:T(8,128)(2,1)S(1)} %copy-done.2, ...), custom_call_target="tpu_custom_call" | custom-call | tf_op jit(solution)/shard_map/pallas_call | solution.py:814
  81.5 1.3 %copy.13 = f32[256,2048]{1,0:T(8,128)} copy(f32[256,2048]{1,0:T(8,128)S(1)} %shard_map.84) | data formatting | bytes 4194304
  (11 shorter events, 0.1 us)
Async XLA Ops:
  0.0 24.9 %copy-start = (f32[16,64,256]{2,1,0:T(8,128)S(1)}, f32[16,64,256]{2,1,0:T(8,128)}, u32[]{:S(2)}) copy-start(f32[16,64,256]{2,1,0:T(8,128)} %constant.93.clone.d_all) | copy-start | bytes 3145732
  3.4 44.9 %copy-start.2 = (bf16[2,128,128]{2,1,0:T(8,128)(2,1)S(1)}, bf16[2,128,128]{2,1,0:T(8,128)(2,1)}, u32[]{:S(2)}) copy-start(bf16[2,128,128]{2,1,0:T(8,128)(2,1)} %constant.95.clone.head_all) | copy-start | bytes 196612
  24.9 23.5 %copy-start.1 = (bf16[2,64,32,64]{3,2,1,0:T(8,128)(2,1)S(1)}, bf16[2,64,32,64]{3,2,1,0:T(8,128)(2,1)}, u32[]{:S(2)}) copy-start(bf16[2,64,32,64]{3,2,1,0:T(8,128)(2,1)} %constant.94.clone.table) | copy-start | bytes 1572868

commit v5 on v4

--- a/solution.py
+++ b/solution.py
@@ -706,11 +706,14 @@
     m_both = jnp.concatenate(
         [m_first + jnp.arange(width), partner * width + jnp.arange(width) - G // 2]
     )[None, :].astype(jnp.float32) * (0.5 / G)
+    given = lax.optimization_barrier(
+        jnp.concatenate([tile_row.reshape(1, blocks), col_offset.reshape(1, blocks)], axis=0)
+    )
     numbers = jnp.stack(
         [
-            tile_row[:, 0],
-            col_offset // SUB,
-            jnp.mod(col_offset, SUB),
+            given[0],
+            given[1] // SUB,
+            jnp.bitwise_and(given[1], SUB - 1),
             jnp.broadcast_to(live_count[0], (blocks,)),
         ]
     )

time: 82.8 us -> 81.7 us (0.987); the launches traced: 82.8 us -> 80.7 us
  Pallas kernels: 77.6 us -> 76 us
    pallas_call x1, Pallas kernels: 33.2 us -> 30.5 us  [on_device(): pl.pallas_call(functools.partial(finish_kernel, width), out_shape=jax.Sha...]
    another operation x3, other arithmetic: 1.4 us -> 0.09 us  [the longest x1 0.07 us: on_device(): jnp.stack([given[0], given[1] // SUB, jnp.bitwise_and(given[1], SUB - 1),...]
    pallas_call x1, Pallas kernels: 23.5 us -> 24.6 us  [on_device(): pl.pallas_call(functools.partial(grid_kernel, width, blocks), out_shape=[...]
where the time goes in v5:
time: 81.7 us; the launch traced here: 80.7 us
  Pallas kernels  76 us (93%)
  other arithmetic  1.92 us (2%)
  local copies, waits for them, and re-layouts  1.85 us (2%)
  between operations  0.89 us (1%)
    pallas_call x1, Pallas kernels, on_device(): pl.pallas_call(functools.partial(finish_kernel, width), out_shape=jax.Sha...  30.5 us
    pallas_call x1, Pallas kernels, on_device(): pl.pallas_call(functools.partial(grid_kernel, width, blocks), out_shape=[...  24.6 us
    pallas_call x1, Pallas kernels, gather_all(): pl.pallas_call(functools.partial(gather_kernel, far, near), out_shape=jax...  21 us

profile of v5, /device:TPU:0, one launch (start us, length us, event | category | flops | bytes accessed | tf_op | source)
XLA Modules:
  0.0 80.7 jit_solution(5752793778887329081)
XLA Ops:
  0.0 0.0 copy-start
  0.7 0.1 pad.19.clone
  0.8 0.1 pad_add_fusion.1.places
  0.9 0.7 pad_add_fusion
  1.6 0.1 maximum_maximum_fusion
  1.7 0.1 lt.24
  1.8 1.0 %pad_maximum_fusion.x_ref = bf16[98,2,256]{2,1,0:T(2,128)(2,1)S(1)} fusion(bf16[2,2,256]{2,1,0:T(2,128)(2,1)S(1)} %reshape.59, bf16[48,2,256]{2,1,0:T(2,128)(2,1)} %param.9, bf16[48,2,256]{2,1,0:T(2,128)(2,1)} %param.8), kind=kLoop, calls=%fused_computation | loop fusion | flops 100352 | bytes 200704 | tf_op jit(solution)/shard_map/concatenate | solution.py:721
  2.8 0.0 copy-start.2
  2.8 21.0 %shard_map.82 = bf16[16,98,2,256]{3,2,1,0:T(2,128)(2,1)S(1)} custom-call(bf16[98,2,256]{2,1,0:T(2,128)(2,1)S(1)} %pad_maximum_fusion.x_ref), custom_call_target="tpu_custom_call" | custom-call | tf_op jit(solution)/shard_map/pallas_call | solution.py:264
  23.8 0.1 slice_reduce_fusion.1
  23.9 0.1 copy.10
  24.0 0.1 squeeze.17
  24.0 0.1 squeeze.18
  24.1 0.1 reshape.60.cols
  24.2 0.0 copy-done
  24.2 0.0 copy-start.1
  24.3 24.6 %shard_map.83 = (bf16[2,64,64,128]{3,2,1,0:T(8,128)(2,1)S(1)}, bf16[2,64,64,128]{3,2,1,0:T(8,128)(2,1)S(1)}) custom-call(s32[768]{0:T(1024)S(1)} %fusion.1.homes, s32[1568]{0:T(1024)S(1)} %reshape.60.cols, s32[16]{0:T(128)S(1)} %bitcast.17, bf16[1568,2,256]{2,1,0:T(2,128)(2,1)S(1)} %bitcast.16, f32[1,512]{1,0:T(1,128)S(1)} %fusion.5.m_ref, ...), custom_call_target="tpu_custom_call" | custom-call | tf_op jit(solution)/shard_map/pallas_call | solution.py:744
  48.9 0.0 copy-done.2
  48.9 0.0 copy-done.1
  48.9 30.5 %shard_map.84 = f32[256,2048]{1,0:T(8,128)S(1)} custom-call(s32[2]{0:T(128)S(1)} %pad_add_fusion.1.places, f32[1]{0:T(128)} %bitcast.2.depths, bf16[2,64,64,128]{3,2,1,0:T(8,128)(2,1)S(1)} %get-tuple-element.7.keep_ref, bf16[2,64,64,128]{3,2,1,0:T(8,128)(2,1)S(1)} %get-tuple-element.8.give_ref, bf16[2,128,128]{2,1,0:T(8,128)(2,1)S(1)} %copy-done.2, ...), custom_call_target="tpu_custom_call" | custom-call | tf_op jit(solution)/shard_map/pallas_call | solution.py:817
  79.4 1.3 %copy.13 = f32[256,2048]{1,0:T(8,128)} copy(f32[256,2048]{1,0:T(8,128)S(1)} %shard_map.84) | data formatting | bytes 4194304
  (13 shorter events, 0.1 us)
Async XLA Ops:
  0.0 24.2 %copy-start = (f32[16,64,256]{2,1,0:T(8,128)S(1)}, f32[16,64,256]{2,1,0:T(8,128)}, u32[]{:S(2)}) copy-start(f32[16,64,256]{2,1,0:T(8,128)} %constant.83.clone.d_all) | copy-start | bytes 3145732
  2.8 46.1 %copy-start.2 = (bf16[2,128,128]{2,1,0:T(8,128)(2,1)S(1)}, bf16[2,128,128]{2,1,0:T(8,128)(2,1)}, u32[]{:S(2)}) copy-start(bf16[2,128,128]{2,1,0:T(8,128)(2,1)} %constant.85.clone.head_all) | copy-start | bytes 196612
  24.2 24.6 %copy-start.1 = (bf16[2,64,32,64]{3,2,1,0:T(8,128)(2,1)S(1)}, bf16[2,64,32,64]{3,2,1,0:T(8,128)(2,1)}, u32[]{:S(2)}) copy-start(bf16[2,64,32,64]{3,2,1,0:T(8,128)(2,1)} %constant.84.clone.table) | copy-start | bytes 1572868

commit v6 on v5

--- a/solution.py
+++ b/solution.py
@@ -19,8 +19,8 @@
 LANES = 128
 PITCH = 129
 OUT_PITCH = 65
-SWAPS = 2
-SENDS = 4
+SWAPS = 4
+SENDS = 8
 plane_step = 6.0
 full_turn = 2.0 * math.pi
 BF = ml_dtypes.bfloat16
@@ -648,7 +648,7 @@
             return carry
 
         for k in range(SENDS):
-            lax.fori_loop(k * step, (k + 1) * step, away_rows, 0, unroll=16)
+            lax.fori_loop(k * step, (k + 1) * step, away_rows, 0, unroll=8)
             at = pl.ds(k * step, step)
             n = c * SENDS + k
             sends.append(
@@ -681,7 +681,7 @@
 
         for k in range(SENDS):
             sends[c * SENDS + k].wait_recv()
-            lax.fori_loop(k * step, (k + 1) * step, add_rows, 0, unroll=16)
+            lax.fori_loop(k * step, (k + 1) * step, add_rows, 0, unroll=8)
 
         for n in range(share // 2):
             rows = [out_t[c, pl.ds((2 * n + h) * OUT_PITCH, 64), :] for h in range(2)]

time: 81.7 us -> 80.7 us (0.988); the launches traced: 80.7 us -> 80.6 us
  no operation moved by 1% of the time
where the time goes in v6:
time: 80.7 us; the launch traced here: 80.6 us
  Pallas kernels  75.9 us (94%)
  other arithmetic  1.92 us (2%)
  local copies, waits for them, and re-layouts  1.85 us (2%)
  between operations  0.89 us (1%)
    pallas_call x1, Pallas kernels, on_device(): pl.pallas_call(functools.partial(finish_kernel, width), out_shape=jax.Sha...  30 us
    pallas_call x1, Pallas kernels, on_device(): pl.pallas_call(functools.partial(grid_kernel, width, blocks), out_shape=[...  24.9 us
    pallas_call x1, Pallas kernels, gather_all(): pl.pallas_call(functools.partial(gather_kernel, far, near), out_shape=jax...  21 us

profile of v6, /device:TPU:0, one launch (start us, length us, event | category | flops | bytes accessed | tf_op | source)
XLA Modules:
  0.0 80.6 jit_solution(8884545588251300723)
XLA Ops:
  0.0 0.0 copy-start
  0.7 0.1 pad.19.clone
  0.8 0.1 pad_add_fusion.1.places
  0.9 0.7 pad_add_fusion
  1.6 0.1 maximum_maximum_fusion
  1.7 0.1 lt.24
  1.8 1.0 %pad_maximum_fusion.x_ref = bf16[98,2,256]{2,1,0:T(2,128)(2,1)S(1)} fusion(bf16[2,2,256]{2,1,0:T(2,128)(2,1)S(1)} %reshape.59, bf16[48,2,256]{2,1,0:T(2,128)(2,1)} %param.9, bf16[48,2,256]{2,1,0:T(2,128)(2,1)} %param.8), kind=kLoop, calls=%fused_computation | loop fusion | flops 100352 | bytes 200704 | tf_op jit(solution)/shard_map/concatenate | solution.py:721
  2.8 0.0 copy-start.2
  2.8 21.0 %shard_map.82 = bf16[16,98,2,256]{3,2,1,0:T(2,128)(2,1)S(1)} custom-call(bf16[98,2,256]{2,1,0:T(2,128)(2,1)S(1)} %pad_maximum_fusion.x_ref), custom_call_target="tpu_custom_call" | custom-call | tf_op jit(solution)/shard_map/pallas_call | solution.py:264
  23.8 0.1 slice_reduce_fusion.1
  23.9 0.1 copy.10
  24.0 0.1 squeeze.17
  24.0 0.1 squeeze.18
  24.1 0.1 reshape.60.cols
  24.2 0.0 copy-done
  24.2 0.0 copy-start.1
  24.3 24.9 %shard_map.83 = (bf16[2,64,64,128]{3,2,1,0:T(8,128)(2,1)S(1)}, bf16[2,64,64,128]{3,2,1,0:T(8,128)(2,1)S(1)}) custom-call(s32[768]{0:T(1024)S(1)} %fusion.1.homes, s32[1568]{0:T(1024)S(1)} %reshape.60.cols, s32[16]{0:T(128)S(1)} %bitcast.17, bf16[1568,2,256]{2,1,0:T(2,128)(2,1)S(1)} %bitcast.16, f32[1,512]{1,0:T(1,128)S(1)} %fusion.5.m_ref, ...), custom_call_target="tpu_custom_call" | custom-call | tf_op jit(solution)/shard_map/pallas_call | solution.py:744
  49.2 0.0 copy-done.2
  49.2 0.0 copy-done.1
  49.2 30.0 %shard_map.84 = f32[256,2048]{1,0:T(8,128)S(1)} custom-call(s32[2]{0:T(128)S(1)} %pad_add_fusion.1.places, f32[1]{0:T(128)} %bitcast.2.depths, bf16[2,64,64,128]{3,2,1,0:T(8,128)(2,1)S(1)} %get-tuple-element.7.keep_ref, bf16[2,64,64,128]{3,2,1,0:T(8,128)(2,1)S(1)} %get-tuple-element.8.give_ref, bf16[2,128,128]{2,1,0:T(8,128)(2,1)S(1)} %copy-done.2, ...), custom_call_target="tpu_custom_call" | custom-call | tf_op jit(solution)/shard_map/pallas_call | solution.py:817
  79.2 1.3 %copy.13 = f32[256,2048]{1,0:T(8,128)} copy(f32[256,2048]{1,0:T(8,128)S(1)} %shard_map.84) | data formatting | bytes 4194304
  (13 shorter events, 0.1 us)
Async XLA Ops:
  0.0 24.2 %copy-start = (f32[16,64,256]{2,1,0:T(8,128)S(1)}, f32[16,64,256]{2,1,0:T(8,128)}, u32[]{:S(2)}) copy-start(f32[16,64,256]{2,1,0:T(8,128)} %constant.83.clone.d_all) | copy-start | bytes 3145732
  2.8 46.4 %copy-start.2 = (bf16[2,128,128]{2,1,0:T(8,128)(2,1)S(1)}, bf16[2,128,128]{2,1,0:T(8,128)(2,1)}, u32[]{:S(2)}) copy-start(bf16[2,128,128]{2,1,0:T(8,128)(2,1)} %constant.85.clone.head_all) | copy-start | bytes 196612
  24.2 25.0 %copy-start.1 = (bf16[2,64,32,64]{3,2,1,0:T(8,128)(2,1)S(1)}, bf16[2,64,32,64]{3,2,1,0:T(8,128)(2,1)}, u32[]{:S(2)}) copy-start(bf16[2,64,32,64]{3,2,1,0:T(8,128)(2,1)} %constant.84.clone.table) | copy-start | bytes 1572868
